TPU v7x, 32 devices: a whole 2x2x4 slice. The times are simulated.
32 devices in a mesh: beams: 2 (over y), tm: 4 (over x, core), band: 4 (over z).
Axes of the slice: x: 2, y: 2, z: 4, core: 2. Of those that a mesh axis runs over, the one named last changes fastest.
Arguments:
- signal: float32 [512, 131072], P(('beams', 'band'), 'tm'), parts along dimension 0, may hold values from -6 to 6
- tree_picks: int32 [2, 8, 256], replicated, may hold values from 0 to 63, as said below
- tree_delays: int32 [8, 256], replicated, may hold values from 0 to 4
- template_bank: float32 [2, 201, 64], replicated, may hold values from -0.75 to 0.75
- template_pick: int32 [8, 64, 2], P(('beams', 'band'), 'tm'), parts along dimension 0, may hold values from 0 to 200
Outputs:
- powers: float32 [8, 64, 2, 65536], P(('beams', 'band'), 'tm'), parts along dimension 0
There are 2 independent parts, one for each index of `beams`. A program takes and returns all parts, laid end to end along the dimension named above; an argument that names none is the same for every part. Nothing has to cross between parts.
Inputs may be any that keep to these rules, and one draw needn't show every extreme that they name: `tree_picks`: entries of section j are below the smaller of 2 to the power j and 64.
All inputs are finite; a program needn't handle non-finite values.
Results may differ from a plain program's by a relative error of at most 0.00007.
Values sent between devices are 32-bit elements; how exact they have to be, the bound alone decides.
A program may use at most 192 MiB of HBM per device.

v0:
```python
import functools
import math

import jax
import jax.numpy as jnp
import ml_dtypes
import numpy as np
from jax import lax
from jax.experimental import pallas as pl
from jax.experimental.pallas import tpu as pltpu
from jax.sharding import PartitionSpec as P

CH_DEV = 64
LOGCD = 6
MAXD = 4
LANES = 128
SUBS = 8
RADIX = 256
LIMIT = 56 * 1024 * 1024


def shifted(value, axis, steps):
    count = lax.axis_size(axis)
    first, last = (max(0, -steps), min(count, count - steps))
    return lax.ppermute(value, axis, [(source, source + steps) for source in range(first, last)])


def tree_kernel(sections, sizes, parts, has_rim, *refs):
    low_ref, high_ref, delay_ref, row_ref = refs[:4]
    xs, refs = refs[4 : 4 + len(parts)], refs[4 + len(parts) :]
    if has_rim:
        rim_ref, refs = refs[0], refs[1:]
    buf_a, buf_b = refs[-2:]
    outs = refs[len(refs) - 2 - len(sizes) : -2]
    rows, _, span = buf_a.shape
    tiles = span // LANES - 1
    lane = lax.broadcasted_iota(jnp.int32, (SUBS, LANES), 1)
    sub = lax.broadcasted_iota(jnp.int32, (SUBS, LANES), 0)

    @pl.loop(0, rows, unroll=4)
    def _(r):
        at = 0
        for x_ref, first in zip(xs, parts):
            count = x_ref.shape[2] - first
            buf_a[r, :, at : at + count] = x_ref[r, :, first:]
            at += count
        if has_rim:
            up = pltpu.roll(xs[0][r, :, 0:LANES], SUBS - 1, 0)
            buf_a[r, :, at : at + LANES] = jnp.where(sub == SUBS - 1, rim_ref[r], up)

    def merge(src, section, r, dst, at, count):
        a = low_ref[section, r]
        b = high_ref[section, r]
        d = delay_ref[section, r]
        turn = (LANES - d) & (LANES - 1)
        keep = lane < LANES - d
        turned = [
            pltpu.roll(src[b, :, i * LANES : (i + 1) * LANES], turn, 1) for i in range(tiles + 1)
        ]
        for i in range(count):
            later = turned[min(i + 1, tiles)]
            dst[at, :, i * LANES : (i + 1) * LANES] = src[
                a, :, i * LANES : (i + 1) * LANES
            ] + jnp.where(keep, turned[i], later)

    src, dst = buf_a, buf_b
    for section in range(sections - 1):

        @pl.loop(0, rows, unroll=16)
        def _(r, src=src, dst=dst, section=section):
            merge(src, section, r, dst, r, tiles + 1)

        src, dst = dst, src
    start = 0
    for size, out in zip(sizes, outs):

        @pl.loop(0, size, unroll=16)
        def _(i, start=start, src=src, out=out):
            merge(src, sections - 1, row_ref[start + i], out, i, tiles)

        start += size


def tree(xs, parts, rim, tables_of, sizes, width, span, place, so_far):
    rows = xs[0].shape[0]
    sections = tables_of[0].shape[0]
    smem = pl.BlockSpec(memory_space=pltpu.SMEM)
    vmem = pl.BlockSpec(memory_space=pltpu.VMEM)
    has_rim = rim is not None
    inputs = [*tables_of, *xs] + ([rim] if has_rim else [])
    known = len(inputs)
    return pl.pallas_call(
        functools.partial(tree_kernel, sections, sizes, parts, has_rim),
        grid=(1,),
        out_shape=[jax.ShapeDtypeStruct((size, SUBS, width), jnp.float32) for size in sizes],
        in_specs=[smem] * 4
        + [vmem] * (known - 4)
        + [pl.BlockSpec(memory_space=pl.ANY)] * len(so_far),
        out_specs=[pl.BlockSpec((size, SUBS, span), lambda i: (0, 0, place)) for size in sizes],
        input_output_aliases={known + i: i for i in range(len(so_far))},
        scratch_shapes=[pltpu.VMEM((rows, SUBS, span + LANES), jnp.float32)] * 2,
        compiler_params=pltpu.CompilerParams(vmem_limit_bytes=LIMIT),
        cost_estimate=pl.CostEstimate(
            flops=rows * SUBS * span * sections * 4,
            bytes_accessed=rows * SUBS * span * 8,
            transcendentals=0,
        ),
        name="tree",
    )(*inputs, *so_far)


def split(value):
    high = value.astype(jnp.bfloat16)
    return high, (value - high.astype(jnp.float32)).astype(jnp.bfloat16)


def bands_kernel(zsel, u_ref, high_ref, low_ref):
    for z in range(zsel):
        pair = []
        for part in range(2):
            row = u_ref[0, 2 * z + part : 2 * z + part + 1, :]
            wide = jnp.broadcast_to(row, (RADIX, RADIX))
            band = pltpu.roll(wide, 0, 1, stride=1, stride_axis=0)[:, :LANES]
            pair.append(split(band))
        at = 2 * z * LANES
        for ref, real, imag in (
            (high_ref, pair[0][0], pair[1][0]),
            (low_ref, pair[0][1], pair[1][1]),
        ):
            ref[0, :RADIX, at : at + LANES] = real
            ref[0, RADIX:, at : at + LANES] = -imag
            ref[0, :RADIX, at + LANES : at + 2 * LANES] = imag
            ref[0, RADIX:, at + LANES : at + 2 * LANES] = real


def bands(picks, template_bank):
    trials, zsel = picks.shape
    taps = template_bank.shape[2]
    onehot = (picks[:, :, None] == jnp.arange(template_bank.shape[1], dtype=jnp.int32)).astype(
        jnp.float32
    )
    reversed_bank = jnp.concatenate(
        [
            template_bank[:, :, :1],
            jnp.zeros(template_bank.shape[:2] + (RADIX - taps,), jnp.float32),
            template_bank[:, :, :0:-1],
        ],
        axis=2,
    )
    u = jnp.einsum("tzk,ckm->tzcm", onehot, reversed_bank, precision=lax.Precision.HIGHEST)
    u = u.reshape(trials, 2 * zsel, RADIX)
    wide = 2 * zsel * LANES
    shape = jax.ShapeDtypeStruct((trials, 2 * RADIX, wide), jnp.bfloat16)
    spec = pl.BlockSpec((1, 2 * RADIX, wide), lambda t: (t, 0, 0))
    return pl.pallas_call(
        functools.partial(bands_kernel, zsel),
        grid=(trials,),
        out_shape=[shape, shape],
        in_specs=[pl.BlockSpec((1, 2 * zsel, RADIX), lambda t: (t, 0, 0))],
        out_specs=[spec, spec],
        compiler_params=pltpu.CompilerParams(vmem_limit_bytes=LIMIT),
        cost_estimate=pl.CostEstimate(
            flops=trials * RADIX * RADIX * 20,
            bytes_accessed=trials * 2 * RADIX * wide * 4,
            transcendentals=0,
        ),
        name="bands",
    )(u)


def tables(samples, channels, width, taps):
    cols = samples // RADIX
    outs = cols // 2
    split_by = width // cols if width % cols == 0 else 1
    place = np.arange(RADIX)
    row_of = split_by * (place % (RADIX // split_by)) + place // (RADIX // split_by)
    freq = (np.arange(RADIX) - taps // 2) % RADIX
    b = np.arange(cols)
    scale = 1.0 / math.sqrt(samples * channels)
    angle = 2.0 * np.pi / RADIX * (row_of[:, None] * freq[None, :] % RADIX)
    first = np.concatenate([np.cos(angle), -np.sin(angle)], axis=1) * scale
    angle = 2.0 * np.pi / samples * (b[:, None] * freq[None, :] % samples)
    tw_cos, tw_sin = np.cos(angle), np.sin(angle)
    angle = 2.0 * np.pi / cols * (np.arange(outs)[:, None] * b[None, :] % cols)
    second = np.concatenate([np.cos(angle), np.sin(angle)], axis=1)

    def parts(value):
        value = value.astype(np.float32)
        high = value.astype(ml_dtypes.bfloat16)
        return high, (value - high.astype(np.float32)).astype(ml_dtypes.bfloat16)

    return (
        *parts(first),
        tw_cos.astype(np.float32),
        tw_sin.astype(np.float32),
        *parts(second),
    )


def dot3(a_high, a_low, b_high, b_low):
    def dot(a, b):
        return jnp.dot(a, b, preferred_element_type=jnp.float32)

    return dot(a_high, b_high) + (dot(a_high, b_low) + dot(a_low, b_high))


def spectra_kernel(zsel, half_taps, aliased, *refs):
    x_ref, bh_ref, bl_ref, fh, fl, tc, ts, sh, sl = refs[:9]
    out_ref, done_ref = refs[10:] if aliased else refs[9:]
    done_ref[...] = jnp.zeros_like(done_ref)
    cols = tc.shape[0]
    outs = cols // 2
    x = x_ref[...]
    x = x.reshape(-1, x.shape[-1])
    if x.shape[1] != cols:
        x = jnp.concatenate(
            [x[:, i * cols : (i + 1) * cols] for i in range(x.shape[1] // cols)], axis=0
        )
    x_high, x_low = split(x.T)
    first = dot3(x_high, x_low, fh[...], fl[...])
    re, im = first[:, :RADIX], first[:, RADIX:]
    mid_re = re * tc[...] + im * ts[...]
    mid_im = im * tc[...] - re * ts[...]
    re_high, re_low = split(mid_re)
    im_high, im_low = split(mid_im)

    def block(a, b):
        return jnp.concatenate(
            [jnp.concatenate([a, b], axis=1), jnp.concatenate([b, -a], axis=1)], axis=0
        )

    spec = dot3(sh[...], sl[...], block(re_high, im_high), block(re_low, im_low))
    row = lax.broadcasted_iota(jnp.int32, (outs, RADIX), 0)
    lane = lax.broadcasted_iota(jnp.int32, (outs, RADIX), 1)
    even, odd = [], []
    for part in (spec[:, :RADIX], spec[:, RADIX:]):
        down = jnp.where(row == 0, 0.0, pltpu.roll(part, 1, 0))
        up = jnp.where(row == outs - 1, 0.0, pltpu.roll(part, outs - 1, 0))
        here = jnp.where(lane < half_taps, down, part)
        after = jnp.where(lane < half_taps, part, up)
        even.append(here)
        odd += [here[:, LANES:], after[:, :LANES]]
    window = jnp.concatenate(
        [jnp.concatenate(even, axis=1), jnp.concatenate(odd, axis=1)], axis=0
    )
    w_high, w_low = split(window)
    got = dot3(w_high, w_low, bh_ref[0], bl_ref[0])
    for z in range(zsel):
        at = 2 * z * LANES
        real, imag = got[:, at : at + LANES], got[:, at + LANES : at + 2 * LANES]
        power = real * real + imag * imag
        for e in range(2):
            out_ref[0, pl.ds(e * zsel + z, outs, 2 * zsel), :] = power[e * outs : (e + 1) * outs]


def spectra(x, band_high, band_low, consts, zsel, taps, trials, first_trial, so_far):
    cols = consts[2].shape[0]
    outs = cols // 2
    rows = 2 * outs * zsel
    if x.shape[-1] % cols == 0:
        here = x.shape[1]
        x_spec = pl.BlockSpec((x.shape[0], 1, SUBS, x.shape[-1]), lambda t: (0, t, 0, 0))
    else:
        here = x.shape[1]
        x = x.transpose(1, 0, 2, 3).reshape(here, RADIX, cols)
        x_spec = pl.BlockSpec((1, RADIX, cols), lambda t: (t, 0, 0))
    band_spec = pl.BlockSpec(
        (1,) + band_high.shape[1:], lambda t: (first_trial + t, 0, 0)
    )
    whole = [pl.BlockSpec(c.shape, lambda t: (0, 0)) for c in consts]
    aliased = so_far is not None
    more = [so_far] if aliased else []
    macs = here * (cols * RADIX * 2 * RADIX + outs * 2 * cols * 2 * RADIX + 2 * outs * 4 * RADIX * RADIX)
    return pl.pallas_call(
        functools.partial(spectra_kernel, zsel, taps // 2, aliased),
        grid=(here,),
        out_shape=[
            jax.ShapeDtypeStruct((trials, rows, LANES), jnp.float32),
            jax.ShapeDtypeStruct((SUBS, LANES), jnp.float32),
        ],
        in_specs=[x_spec, band_spec, band_spec, *whole]
        + [pl.BlockSpec(memory_space=pl.ANY)] * len(more),
        out_specs=[
            pl.BlockSpec((1, rows, LANES), lambda t: (first_trial + t, 0, 0)),
            pl.BlockSpec((SUBS, LANES), lambda t: (0, 0)),
        ],
        input_output_aliases={9: 0} if aliased else {},
        compiler_params=pltpu.CompilerParams(vmem_limit_bytes=LIMIT),
        cost_estimate=pl.CostEstimate(
            flops=6 * macs, bytes_accessed=here * 2 * 1024 * 1024, transcendentals=0
        ),
        name="spectra",
    )(x, band_high, band_low, *consts, *more)


def after_kernel(value_ref, done_ref, out_ref):
    del value_ref, done_ref, out_ref


def after(value, done):
    anywhere = pl.BlockSpec(memory_space=pl.ANY)
    return pl.pallas_call(
        after_kernel,
        out_shape=jax.ShapeDtypeStruct(value.shape, value.dtype),
        in_specs=[anywhere, anywhere],
        out_specs=anywhere,
        input_output_aliases={0: 0},
        name="after",
    )(value, done)


def on_device(signal, tree_picks, tree_delays, template_bank, template_pick):
    band_count = lax.axis_size("band")
    time_count = lax.axis_size("tm")
    everyone = band_count * time_count
    sections = LOGCD + band_count.bit_length() - 1
    rim_depth = sections * MAXD
    channels = CH_DEV * band_count
    samples = signal.shape[1] * time_count
    slab = signal.shape[1] // band_count
    width = slab // SUBS
    trials = CH_DEV // time_count
    last = max(1, 3 * trials // 16)
    counts = [count for count in (trials - last, last) if count]
    zsel = template_pick.shape[2]
    taps = template_bank.shape[2]

    band_high, band_low = bands(template_pick[0], template_bank)

    half = (1 << np.arange(sections))[:, None]
    r = np.arange(channels)[None, :]
    base = r - r % (2 * half) + r % half - r % np.minimum(half, CH_DEV)
    low = tree_picks[0] + base.astype(np.int32)
    high = tree_picks[1] + (base + half).astype(np.int32)
    grid = np.arange(channels).reshape(band_count, time_count, trials).transpose(1, 0, 2)
    firsts = [sum(counts[:q]) for q in range(len(counts))]
    order = np.concatenate(
        [grid[:, :, first : first + count].reshape(-1) for first, count in zip(firsts, counts)]
    ).astype(np.int32)
    tables_of = (low, high, tree_delays, jnp.asarray(order))
    sizes = [everyone * count for count in counts]

    folded = signal.reshape(CH_DEV, band_count, SUBS, width)

    def exchanged(value):
        value = lax.all_to_all(value, "band", split_axis=0, concat_axis=0, tiled=True)
        return value.reshape(channels, SUBS, -1)

    def rim_of(x):
        rim = shifted(x[:, 0, :rim_depth], ("tm", "band"), -1)
        rim = jnp.pad(rim, ((0, 0), (0, LANES - rim_depth)))
        return jnp.broadcast_to(rim[:, None, :], (channels, SUBS, LANES))

    if width % (2 * LANES) == 0:
        span = width // 2
        cut = span + LANES
        x_a = exchanged(folded[..., :cut].transpose(1, 0, 2, 3))
        x_b = after(after(folded[..., cut:].transpose(1, 0, 2, 3), x_a), band_low)
        x_b = exchanged(x_b)
        pieces = tree([x_a], [0], None, tables_of, sizes, width, span, 0, [])
        pieces = tree(
            [x_a, x_b], [span, 0], rim_of(x_a), tables_of, sizes, width, span, 1, pieces
        )
    else:
        x = exchanged(folded.transpose(1, 0, 2, 3))
        pieces = tree([x], [0], rim_of(x), tables_of, sizes, width, width, 0, [])

    consts = [jnp.asarray(c) for c in tables(samples, channels, width, taps)]
    out = None
    for first, count, piece in zip(firsts, counts, pieces):
        piece = piece.reshape(everyone, count, SUBS, width)
        if out is not None:
            piece = after(piece, arrived)
        arrived = lax.all_to_all(piece, ("tm", "band"), split_axis=0, concat_axis=0, tiled=True)
        out, _ = spectra(
            arrived, band_high, band_low, consts, zsel, taps, trials, first, out
        )
    out = out.reshape(trials, samples // 2 // LANES, zsel, LANES).transpose(0, 2, 1, 3)
    return out.reshape(1, trials, zsel, samples // 2)


def solution(mesh):
    in_specs = (P(("beams", "band"), "tm"), P(), P(), P(), P(("beams", "band"), "tm", None))
    out_specs = P(("beams", "band"), "tm", None, None)
    return jax.shard_map(
        on_device, mesh=mesh, in_specs=in_specs, out_specs=out_specs, check_vma=False
    )
```

profile of v0, /device:TPU:0, one launch (start us, length us, event | category | flops | bytes accessed | tf_op | source)
XLA Modules:
  0.0 449.9 jit_solution(6023776304432600187)
XLA Ops:
  0.0 8.1 %copy.41 = f32[8,8,32,1024]{3,2,1,0:T(8,128)S(1)} copy(f32[8,8,32,1024]{3,1,2,0:T(8,128)} %bitcast.36) | data formatting | bytes 16777216
  8.1 0.0 copy-start
  8.1 0.6 slice_bitcast_fusion
  8.8 2.7 copy-done
  11.5 2.7 copy.31
  14.2 0.0 copy-start.3
  14.2 0.0 copy-start.7
  14.2 6.4 %all-to-all-start = ((f32[4,64,8,640]{3,2,1,0:T(8,128)}), f32[4,64,8,640]{3,2,1,0:T(8,128)}, u32[]{:S(2)}, u32[]{:S(2)}) async-start(f32[4,64,8,640]{3,2,1,0:T(8,128)} %copy.31), calls=%async_computation | async-start | bytes 10485760 | tf_op jit(solution)/shard_map/all_to_all | solution.py:346
  20.7 0.0 copy-done.3
  20.7 0.1 copy.40
  20.8 0.7 rev.3
  21.5 0.1 copy.34
  21.6 0.1 pad.6.clone
  21.7 0.0 copy-done.7
  21.7 0.3 fusion
  22.1 0.7 copy.38.u_ref
  22.7 11.2 %bands.1 = (bf16[16,512,512]{2,1,0:T(8,128)(2,1)}, bf16[16,512,512]{2,1,0:T(8,128)(2,1)}) custom-call(f32[16,4,256]{2,1,0:T(4,128)} %copy.38.u_ref), custom_call_target="tpu_custom_call" | custom-call | flops 20971520 | bytes 16777216 | tf_op jit(solution)/shard_map/bands/pallas_call | solution.py:155
  34.0 3.9 copy_bitcast_fusion.value_ref
  37.8 98.9 %all-to-all-done = f32[4,64,8,640]{3,2,1,0:T(8,128)} async-done(((f32[4,64,8,640]{3,2,1,0:T(8,128)}), f32[4,64,8,640]{3,2,1,0:T(8,128)}, u32[]{:S(2)}, u32[]{:S(2)}) %all-to-all-start) | async-done | bytes 5242912 | tf_op jit(solution)/shard_map/all_to_all | solution.py:346
  136.7 0.0 copy-start.4
  136.8 0.0 copy-start.5
  136.8 0.0 copy-start.6
  136.8 3.8 all-to-all-start.1
  140.6 1.3 slice.30
  141.9 1.3 collective-permute-start
  143.2 0.0 copy-done.4
  143.2 0.0 copy-done.5
  143.2 0.0 copy-done.6
  143.2 0.6 add_bitcast_fusion
  143.8 24.8 %tree.2 = (f32[208,8,1024]{2,1,0:T(8,128)}, f32[48,8,1024]{2,1,0:T(8,128)}) custom-call(s32[8,256]{1,0:T(8,128)} %get-tuple-element.22.refs_0_, s32[8,256]{1,0:T(8,128)} %get-tuple-element.21.refs_1_, s32[8,256]{1,0:T(8,128)} %refs_2_.3, s32[256]{0:T(256)} %constant.24.clone.refs_3_, f32[256,8,640]{2,1,0:T(8,128)} %bitcast.3.done_ref.refs_4_), custom_call_target="tpu_custom_call" | custom-call | flops 33554432 | bytes 8388608 | tf_op jit(solution)/shard_map/tree/pallas_call | solution.py:92
  168.7 11.3 %collective-permute-done = f32[256,32]{1,0:T(8,128)S(1)} collective-permute-done((f32[256,32]{1,0:T(8,128)S(1)}, f32[256,32]{1,0:T(8,128)S(1)}, u32[]{:S(2)}, u32[]{:S(2)}) %collective-permute-start) | collective-permute-done | bytes 32800 | tf_op jit(solution)/shard_map/ppermute | solution.py:25
  180.0 31.8 %all-to-all-done.1 = f32[4,64,8,384]{3,2,1,0:T(8,128)S(1)} async-done(((f32[4,64,8,384]{3,2,1,0:T(8,128)}), f32[4,64,8,384]{3,2,1,0:T(8,128)S(1)}, u32[]{:S(2)}, u32[]{:S(2)}) %all-to-all-start.1) | async-done | bytes 3145760 | tf_op jit(solution)/shard_map/all_to_all | solution.py:346
  211.8 0.0 copy-start.1
  211.8 1.1 broadcast_in_dim.5.refs_6_
  213.0 0.9 copy-done.1
  213.8 26.1 %tree.3 = (f32[208,8,1024]{2,1,0:T(8,128)}, f32[48,8,1024]{2,1,0:T(8,128)}) custom-call(s32[8,256]{1,0:T(8,128)} %get-tuple-element.22.refs_0_, s32[8,256]{1,0:T(8,128)} %get-tuple-element.21.refs_1_, s32[8,256]{1,0:T(8,128)} %refs_2_.3, s32[256]{0:T(256)} %constant.24.clone.refs_3_, ...), custom_call_target="tpu_custom_call", output_to_operand_aliasing={{0}: (7, {}), {1}: (8, {})} | custom-call | flops 33554432 | bytes 8388608 | tf_op jit(solution)/shard_map/tree/pallas_call | solution.py:92
  239.9 156.3 %all_to_all.20.done_ref.refs_0_ = f32[16,13,8,1024]{3,2,1,0:T(8,128)} all-to-all(f32[16,13,8,1024]{3,2,1,0:T(8,128)} %bitcast.33), channel_id=1, replica_groups=mesh['beams'=2,'tm'=4,'band'=4] {'tm','band'}, dimensions={0} | all-to-all | bytes 13631488 | tf_op jit(solution)/shard_map/all_to_all | solution.py:374
  396.2 3.9 all-to-all-start.3
  400.1 35.9 %spectra.2 = (f32[16,1024,128]{2,1,0:T(8,128)}, f32[8,128]{1,0:T(8,128)}) custom-call(f32[16,13,8,1024]{3,2,1,0:T(8,128)} %all_to_all.20.done_ref.refs_0_, bf16[16,512,512]{2,1,0:T(8,128)(2,1)} %get-tuple-element.18.refs_1_, bf16[16,512,512]{2,1,0:T(8,128)(2,1)} %get-tuple-element.13.done_ref.refs_2_, bf16[256,512]{1,0:T(8,128)(2,1)} %constant.25.clone.refs_3_, ...), custom_call_target="tpu_custom_call" | custom-call | flops 26172456960 | bytes 27262976 | tf_op jit(solution)/shard_map/spectra/pallas_call | solution.py:274
  436.1 2.0 all-to-all-done.3.refs_0_
  438.1 0.0 copy-start.2
  438.1 1.2 copy-done.2
  439.3 10.6 %spectra.3 = (f32[16,1024,128]{2,1,0:T(8,128)}, f32[8,128]{1,0:T(8,128)}) custom-call(f32[16,3,8,1024]{3,2,1,0:T(8,128)} %copy-done.2, bf16[16,512,512]{2,1,0:T(8,128)(2,1)} %get-tuple-element.18.refs_1_, bf16[16,512,512]{2,1,0:T(8,128)(2,1)} %get-tuple-element.13.done_ref.refs_2_, ...), custom_call_target="tpu_custom_call", output_to_operand_aliasing={{0}: (9, {})} | custom-call | flops 6039797760 | bytes 6291456 | tf_op jit(solution)/shard_map/spectra/pallas_call | solution.py:274
  (7 shorter events, 0.0 us)
Async XLA Ops:
  8.1 3.4 copy-start
  14.2 6.5 %copy-start.3 = (f32[2,201,64]{1,2,0:T(8,128)S(1)}, f32[2,201,64]{1,2,0:T(8,128)}, u32[]{:S(2)}) copy-start(f32[2,201,64]{1,2,0:T(8,128)} %param.17) | copy-start | bytes 308740
  14.2 7.5 %copy-start.7 = (s32[1,16,2]{1,2,0:T(2,128)S(1)}, s32[1,16,2]{1,2,0:T(2,128)}, u32[]{:S(2)}) copy-start(s32[1,16,2]{1,2,0:T(2,128)} %param.18) | copy-start | bytes 388
  14.2 122.5 %all-to-all-start = ((f32[4,64,8,640]{3,2,1,0:T(8,128)}), f32[4,64,8,640]{3,2,1,0:T(8,128)}, u32[]{:S(2)}, u32[]{:S(2)}) async-start(f32[4,64,8,640]{3,2,1,0:T(8,128)} %copy.31), calls=%async_computation | async-start | bytes 10485760 | tf_op jit(solution)/shard_map/all_to_all | solution.py:346
  136.7 6.5 %copy-start.4 = (s32[2,8,256]{2,1,0:T(8,128)S(1)}, s32[2,8,256]{2,1,0:T(8,128)}, u32[]{:S(2)}) copy-start(s32[2,8,256]{2,1,0:T(8,128)} %param.15) | copy-start | bytes 49156
  136.8 6.5 %copy-start.5 = (s32[1,8,256]{2,1,0:T(8,128)S(1)}, s32[1,8,256]{2,1,0:T(8,128)}, u32[]{:S(2)}) copy-start(s32[1,8,256]{2,1,0:T(8,128)} %constant.35) | copy-start | bytes 24580
  136.8 6.5 %copy-start.6 = (s32[1,8,256]{2,1,0:T(8,128)S(1)}, s32[1,8,256]{2,1,0:T(8,128)}, u32[]{:S(2)}) copy-start(s32[1,8,256]{2,1,0:T(8,128)} %constant.34) | copy-start | bytes 24580
  136.8 75.1 %all-to-all-start.1 = ((f32[4,64,8,384]{3,2,1,0:T(8,128)}), f32[4,64,8,384]{3,2,1,0:T(8,128)S(1)}, u32[]{:S(2)}, u32[]{:S(2)}) async-start(f32[4,64,8,384]{3,2,1,0:T(8,128)} %after.4), calls=%async_computation.1 | async-start | bytes 6291456 | tf_op jit(solution)/shard_map/all_to_all | solution.py:346
  141.9 38.1 %collective-permute-start = (f32[256,32]{1,0:T(8,128)S(1)}, f32[256,32]{1,0:T(8,128)S(1)}, u32[]{:S(2)}, u32[]{:S(2)}) collective-permute-start(f32[256,32]{1,0:T(8,128)S(1)} %bitcast.38), channel_id=1, source_target_pairs={{1,0},{2,1},{3,2},{4,3},{5,4},{6,5},{7,6},{8,7},{9,8},{10,9},{11,1... | collective-permute-start | bytes 98312 | tf_op jit(solution)/shard_map/ppermute | solution.py:25
  211.8 2.0 copy-start.1
  396.2 41.9 %all-to-all-start.3 = ((f32[16,3,8,1024]{3,2,1,0:T(8,128)}), f32[16,3,8,1024]{3,2,1,0:T(8,128)S(1)}, u32[]{:S(2)}, u32[]{:S(2)}) async-start(f32[16,3,8,1024]{3,2,1,0:T(8,128)} %after.5), calls=%async_computation.3 | async-start | bytes 3145728 | tf_op jit(solution)/shard_map/all_to_all | solution.py:374
  438.1 1.2 copy-start.2
where the time goes:
time: 451 us; the launch traced here: 450 us
  blocking collectives  156 us (35%)
  waiting for transfers between devices  144 us (32%)
  Pallas kernels  109 us (24%)
  local copies, waits for them, and re-layouts  24.3 us (5%)
  starting transfers between devices  15.5 us (3%)
    all_to_all x1, blocking collectives, on_device(): lax.all_to_all(piece, ('tm', 'band'), split_axis=0, concat_axis=0, tiled=...  156 us
    all_to_all x2, waiting for transfers between devices, exchanged(): lax.all_to_all(value, 'band', split_axis=0, concat_axis=0, tiled=True)  131 us
    pallas_call x2, Pallas kernels, tree(): pl.pallas_call(functools.partial(tree_kernel, sections, sizes, parts, has...  50.9 us
    pallas_call x2, Pallas kernels, spectra(): pl.pallas_call(functools.partial(spectra_kernel, zsel, taps // 2, aliased...  46.6 us
    unnamed x18, local copies, waits for them, and re-layouts  13.1 us
    ppermute x1, waiting for transfers between devices, shifted(): lax.ppermute(value, axis, [(source, source + steps) for source in range(f...  11.3 us
    pallas_call x1, Pallas kernels, bands(): pl.pallas_call(functools.partial(bands_kernel, zsel), grid=(trials,), out...  11.2 us
    all_to_all x2, starting transfers between devices, exchanged(): lax.all_to_all(value, 'band', split_axis=0, concat_axis=0, tiled=True)  10.3 us
  transfers between devices with their start and end apart: 4, of which 4 were waited for; matrix products, arithmetic and copies ran while one was open for 2% of the time, Pallas kernels for 16%

commit v1 on v0

--- a/solution.py
+++ b/solution.py
@@ -17,6 +17,10 @@
 SUBS = 8
 RADIX = 256
 LIMIT = 56 * 1024 * 1024
+FUSED_LIMIT = 62 * 1024 * 1024
+GROUP = 2
+AHEAD = 3
+MESH = pl.DeviceIdType.MESH
 
 
 def shifted(value, axis, steps):
@@ -114,11 +118,11 @@
     return high, (value - high.astype(jnp.float32)).astype(jnp.bfloat16)
 
 
-def bands_kernel(zsel, u_ref, high_ref, low_ref):
+def fill_bands(u, zsel, high_ref, low_ref):
     for z in range(zsel):
         pair = []
         for part in range(2):
-            row = u_ref[0, 2 * z + part : 2 * z + part + 1, :]
+            row = u[2 * z + part : 2 * z + part + 1, :]
             wide = jnp.broadcast_to(row, (RADIX, RADIX))
             band = pltpu.roll(wide, 0, 1, stride=1, stride_axis=0)[:, :LANES]
             pair.append(split(band))
@@ -127,13 +131,17 @@
             (high_ref, pair[0][0], pair[1][0]),
             (low_ref, pair[0][1], pair[1][1]),
         ):
-            ref[0, :RADIX, at : at + LANES] = real
-            ref[0, RADIX:, at : at + LANES] = -imag
-            ref[0, :RADIX, at + LANES : at + 2 * LANES] = imag
-            ref[0, RADIX:, at + LANES : at + 2 * LANES] = real
-
-
-def bands(picks, template_bank):
+            ref[:RADIX, at : at + LANES] = real
+            ref[RADIX:, at : at + LANES] = -imag
+            ref[:RADIX, at + LANES : at + 2 * LANES] = imag
+            ref[RADIX:, at + LANES : at + 2 * LANES] = real
+
+
+def bands_kernel(zsel, u_ref, high_ref, low_ref):
+    fill_bands(u_ref[0], zsel, high_ref.at[0], low_ref.at[0])
+
+
+def reversed_taps(picks, template_bank):
     trials, zsel = picks.shape
     taps = template_bank.shape[2]
     onehot = (picks[:, :, None] == jnp.arange(template_bank.shape[1], dtype=jnp.int32)).astype(
@@ -148,7 +156,12 @@
         axis=2,
     )
     u = jnp.einsum("tzk,ckm->tzcm", onehot, reversed_bank, precision=lax.Precision.HIGHEST)
-    u = u.reshape(trials, 2 * zsel, RADIX)
+    return u.reshape(trials, 2 * zsel, RADIX)
+
+
+def bands(picks, template_bank):
+    trials, zsel = picks.shape
+    u = reversed_taps(picks, template_bank)
     wide = 2 * zsel * LANES
     shape = jax.ShapeDtypeStruct((trials, 2 * RADIX, wide), jnp.bfloat16)
     spec = pl.BlockSpec((1, 2 * RADIX, wide), lambda t: (t, 0, 0))
@@ -204,18 +217,10 @@
     return dot(a_high, b_high) + (dot(a_high, b_low) + dot(a_low, b_high))
 
 
-def spectra_kernel(zsel, half_taps, aliased, *refs):
-    x_ref, bh_ref, bl_ref, fh, fl, tc, ts, sh, sl = refs[:9]
-    out_ref, done_ref = refs[10:] if aliased else refs[9:]
-    done_ref[...] = jnp.zeros_like(done_ref)
+def powers_of(x, band_high, band_low, consts, zsel, half_taps, store):
+    fh, fl, tc, ts, sh, sl = consts
     cols = tc.shape[0]
     outs = cols // 2
-    x = x_ref[...]
-    x = x.reshape(-1, x.shape[-1])
-    if x.shape[1] != cols:
-        x = jnp.concatenate(
-            [x[:, i * cols : (i + 1) * cols] for i in range(x.shape[1] // cols)], axis=0
-        )
     x_high, x_low = split(x.T)
     first = dot3(x_high, x_low, fh[...], fl[...])
     re, im = first[:, :RADIX], first[:, RADIX:]
@@ -244,13 +249,32 @@
         [jnp.concatenate(even, axis=1), jnp.concatenate(odd, axis=1)], axis=0
     )
     w_high, w_low = split(window)
-    got = dot3(w_high, w_low, bh_ref[0], bl_ref[0])
+    got = dot3(w_high, w_low, band_high, band_low)
     for z in range(zsel):
         at = 2 * z * LANES
         real, imag = got[:, at : at + LANES], got[:, at + LANES : at + 2 * LANES]
         power = real * real + imag * imag
         for e in range(2):
-            out_ref[0, pl.ds(e * zsel + z, outs, 2 * zsel), :] = power[e * outs : (e + 1) * outs]
+            store(pl.ds(e * zsel + z, outs, 2 * zsel), power[e * outs : (e + 1) * outs])
+
+
+def spectra_kernel(zsel, half_taps, aliased, *refs):
+    x_ref, bh_ref, bl_ref = refs[:3]
+    consts = refs[3:9]
+    out_ref, done_ref = refs[10:] if aliased else refs[9:]
+    done_ref[...] = jnp.zeros_like(done_ref)
+    cols = consts[2].shape[0]
+    x = x_ref[...]
+    x = x.reshape(-1, x.shape[-1])
+    if x.shape[1] != cols:
+        x = jnp.concatenate(
+            [x[:, i * cols : (i + 1) * cols] for i in range(x.shape[1] // cols)], axis=0
+        )
+
+    def store(rows, value):
+        out_ref[0, rows, :] = value
+
+    powers_of(x, bh_ref[0], bl_ref[0], consts, zsel, half_taps, store)
 
 
 def spectra(x, band_high, band_low, consts, zsel, taps, trials, first_trial, so_far):
@@ -309,6 +333,329 @@
     )(value, done)
 
 
+def finish(out, trials, samples, zsel):
+    out = out.reshape(trials, samples // 2 // LANES, zsel, LANES).transpose(0, 2, 1, 3)
+    return out.reshape(1, trials, zsel, samples // 2)
+
+
+def fused_kernel(
+    nb, nt, sections, trials, zsel, taps,
+    picks_ref, delay_ref, u_ref, sig_ref, *refs
+):
+    const_refs, refs = refs[:6], refs[6:]
+    out_ref, refs = refs[0], refs[1:]
+    raw, refs = refs[0], refs[1:]
+    rim, buf_a, buf_b = refs[:3]
+    sent, got, refs = refs[3:5], refs[5:7], refs[7:]
+    band_high, band_low, power, refs = refs[0], refs[1], refs[2], refs[3:]
+    consts, refs = refs[:6], refs[6:]
+    one_send, one_recv, two_send, two_recv, rim_sems, own_one, own_two, const_sems, out_sems = refs
+
+    everyone = nb * nt
+    rows, _, span = buf_a.shape
+    span = span - LANES
+    blocks = CH_DEV // SUBS
+    groups = trials // GROUP
+    tiles = span // LANES
+    early = range(tiles + 1)
+    late = range(tiles + 1, 2 * tiles)
+    mt, mb = lax.axis_index("tm"), lax.axis_index("band")
+    me = mt * nb + mb
+
+    def device(e):
+        return {"tm": e // nb, "band": e % nb}
+
+    barrier = pltpu.get_barrier_semaphore()
+
+    @pl.loop(1, everyone)
+    def _(d):
+        pl.semaphore_signal(
+            barrier, 1, device_id=device((me + d) % everyone), device_id_type=MESH
+        )
+
+    pl.semaphore_wait(barrier, everyone - 1)
+
+    def slab(i, k):
+        return sig_ref.at[:, k, :, pl.ds(i * LANES, LANES)]
+
+    def first(i, d):
+        return pltpu.make_async_remote_copy(
+            slab(i, (mb + d) % nb),
+            raw.at[pl.ds(mb * blocks, blocks), i],
+            one_send.at[i, d - 1],
+            one_recv.at[i, d - 1],
+            device_id={"band": (mb + d) % nb},
+            device_id_type=MESH,
+        )
+
+    def first_from(i, d):
+        source = (mb + nb - d) % nb
+        return pltpu.make_async_remote_copy(
+            slab(i, mb),
+            raw.at[pl.ds(source * blocks, blocks), i],
+            one_send.at[i, d - 1],
+            one_recv.at[i, d - 1],
+            device_id={"band": source},
+            device_id_type=MESH,
+        )
+
+    def first_own(i):
+        return pltpu.make_async_copy(
+            slab(i, mb), raw.at[pl.ds(mb * blocks, blocks), i], own_one.at[i]
+        )
+
+    def first_wait(i):
+        for d in range(1, nb):
+            first_from(i, d).wait_recv()
+        first_own(i).wait()
+
+    apart = sorted(range(1, nb), key=lambda d: -min(d, nb - d))
+    for i in (*early, *late):
+        for d in apart:
+            first(i, d).start()
+        first_own(i).start()
+    loads = [
+        pltpu.make_async_copy(a, b, const_sems.at[i])
+        for i, (a, b) in enumerate(zip(const_refs, consts))
+    ]
+    for load in loads:
+        load.start()
+
+    lane = lax.broadcasted_iota(jnp.int32, (SUBS, LANES), 1)
+    sub = lax.broadcasted_iota(jnp.int32, (SUBS, LANES), 0)
+
+    def merge(src, section, r, dst, at, count):
+        half = 1 << section
+        base = r - r % (2 * half) + r % half - r % min(half, CH_DEV)
+        a = base + picks_ref[0, section, r]
+        b = base + half + picks_ref[1, section, r]
+        d = delay_ref[section, r]
+        turn = (LANES - d) & (LANES - 1)
+        keep = lane < LANES - d
+        turned = [
+            pltpu.roll(src[b, :, i * LANES : (i + 1) * LANES], turn, 1) for i in range(tiles + 1)
+        ]
+        for i in range(count):
+            later = turned[min(i + 1, tiles)]
+            dst[at, :, i * LANES : (i + 1) * LANES] = src[
+                a, :, i * LANES : (i + 1) * LANES
+            ] + jnp.where(keep, turned[i], later)
+
+    def tree_part(c):
+        @pl.loop(0, nb * blocks)
+        def _(q):
+            for ch in range(SUBS):
+                r = q * SUBS + ch
+                rows_of = pl.ds(ch, SUBS, stride=SUBS)
+                for i in range(tiles + 1 - c):
+                    buf_a[r, :, i * LANES : (i + 1) * LANES] = raw[q, c * tiles + i, rows_of, :]
+                if c == 1:
+                    up = pltpu.roll(raw[q, 0, rows_of, :], SUBS - 1, 0)
+                    edge = jnp.broadcast_to(rim[q, ch : ch + 1, :], (SUBS, LANES))
+                    buf_a[r, :, span:] = jnp.where(sub == SUBS - 1, edge, up)
+
+        src, dst = buf_a, buf_b
+        for section in range(sections - 1):
+
+            @pl.loop(0, rows, unroll=16)
+            def _(r, src=src, dst=dst, section=section):
+                merge(src, section, r, dst, r, tiles + 1)
+
+            src, dst = dst, src
+
+        @pl.loop(0, everyone)
+        def _(e):
+            start = (e % nb) * CH_DEV + (e // nb) * trials
+
+            @pl.loop(0, trials, unroll=trials)
+            def _(i):
+                merge(src, sections - 1, start + i, sent[c].at[e], i, tiles)
+
+    def second(c, g, d):
+        e = (me + d) % everyone
+        which = pl.ds(g * GROUP, GROUP) if c else slice(None)
+        at = 1 + g if c else 0
+        return pltpu.make_async_remote_copy(
+            sent[c].at[e, which],
+            got[c].at[me, which],
+            two_send.at[at, d - 1],
+            two_recv.at[at, d - 1],
+            device_id=device(e),
+            device_id_type=MESH,
+        )
+
+    def second_from(c, g, d):
+        e = (me + everyone - d) % everyone
+        which = pl.ds(g * GROUP, GROUP) if c else slice(None)
+        at = 1 + g if c else 0
+        return pltpu.make_async_remote_copy(
+            sent[c].at[e, which],
+            got[c].at[e, which],
+            two_send.at[at, d - 1],
+            two_recv.at[at, d - 1],
+            device_id=device(e),
+            device_id_type=MESH,
+        )
+
+    def second_own(c):
+        return pltpu.make_async_copy(sent[c].at[me], got[c].at[me], own_two.at[c])
+
+    def send_second(c, g):
+        @pl.loop(1, everyone)
+        def _(d):
+            second(c, g, d).start()
+
+    for i in early:
+        first_wait(i)
+    rim_copy = pltpu.make_async_remote_copy(
+        raw.at[:, 0, pl.ds(0, SUBS)],
+        rim,
+        rim_sems.at[0],
+        rim_sems.at[1],
+        device_id=device((me + everyone - 1) % everyone),
+        device_id_type=MESH,
+    )
+
+    @pl.when(me > 0)
+    def _():
+        rim_copy.start()
+
+    @pl.when(me == everyone - 1)
+    def _():
+        rim[...] = jnp.zeros_like(rim)
+
+    tree_part(0)
+    send_second(0, 0)
+    second_own(0).start()
+    for i in late:
+        first_wait(i)
+
+    @pl.when(me < everyone - 1)
+    def _():
+        rim_copy.wait_recv()
+
+    tree_part(1)
+    second_own(1).start()
+    for g in range(min(AHEAD, groups)):
+        send_second(1, g)
+    for i in (*early, *late):
+        for d in range(1, nb):
+            first(i, d).wait_send()
+
+    @pl.when(me > 0)
+    def _():
+        rim_copy.wait_send()
+
+    for load in loads:
+        load.wait()
+    second_own(0).wait()
+    second_own(1).wait()
+
+    @pl.loop(1, everyone)
+    def _(d):
+        second_from(0, 0, d).wait_recv()
+        second(0, 0, d).wait_send()
+
+    cols = consts[2].shape[0]
+
+    def out_copy(t, j):
+        return pltpu.make_async_copy(power.at[j], out_ref.at[t], out_sems.at[j])
+
+    @pl.loop(0, groups)
+    def _(g):
+        for j in range(GROUP):
+            fill_bands(u_ref[g * GROUP + j], zsel, band_high.at[j], band_low.at[j])
+
+        @pl.loop(1, everyone)
+        def _(d):
+            second_from(1, g, d).wait_recv()
+            second(1, g, d).wait_send()
+
+        @pl.when(g + AHEAD < groups)
+        def _():
+            send_second(1, g + AHEAD)
+
+        for j in range(GROUP):
+            t = g * GROUP + j
+            parts = [got[c][:, t].reshape(everyone * SUBS, span) for c in range(2)]
+            x = jnp.concatenate(
+                [part[:, i : i + cols] for part in parts for i in range(0, span, cols)], axis=0
+            )
+
+            @pl.when(g > 0)
+            def _(j=j, t=t):
+                out_copy(t - GROUP, j).wait()
+
+            def store(where, value, j=j):
+                power[j, where, :] = value
+
+            powers_of(x, band_high[j], band_low[j], consts, zsel, taps // 2, store)
+            out_copy(t, j).start()
+
+    for j in range(GROUP):
+        out_copy(trials - GROUP + j, j).wait()
+
+
+def fused(signal, picks, delays, u, consts, zsel, taps, nb, nt):
+    sections = picks.shape[1]
+    channels = CH_DEV * nb
+    everyone = nb * nt
+    trials = CH_DEV // nt
+    slab = signal.shape[1] // nb
+    width = slab // SUBS
+    span = width // 2
+    blocks = CH_DEV // SUBS
+    cols = consts[2].shape[0]
+    outs = cols // 2
+    rows = 2 * outs * zsel
+    groups = trials // GROUP
+    wide = 2 * zsel * LANES
+    view = signal.reshape(blocks, SUBS, nb * SUBS, width).transpose(0, 2, 1, 3)
+    view = view.reshape(blocks, nb, SUBS * SUBS, width)
+    smem = pl.BlockSpec(memory_space=pltpu.SMEM)
+    vmem = pl.BlockSpec(memory_space=pltpu.VMEM)
+    anywhere = pl.BlockSpec(memory_space=pl.ANY)
+    dma = pltpu.SemaphoreType.DMA
+    f32 = jnp.float32
+    macs = trials * (cols * RADIX * 2 * RADIX + outs * 2 * cols * 2 * RADIX + 2 * outs * 4 * RADIX * RADIX)
+    return pl.pallas_call(
+        functools.partial(fused_kernel, nb, nt, sections, trials, zsel, taps),
+        out_shape=jax.ShapeDtypeStruct((trials, rows, LANES), f32),
+        in_specs=[smem, smem, vmem] + [anywhere] * 7,
+        out_specs=anywhere,
+        scratch_shapes=[
+            pltpu.VMEM((nb * blocks, width // LANES, SUBS * SUBS, LANES), f32),
+            pltpu.VMEM((nb * blocks, SUBS, LANES), f32),
+            pltpu.VMEM((channels, SUBS, span + LANES), f32),
+            pltpu.VMEM((channels, SUBS, span + LANES), f32),
+            pltpu.VMEM((everyone, trials, SUBS, span), f32),
+            pltpu.VMEM((everyone, trials, SUBS, span), f32),
+            pltpu.VMEM((everyone, trials, SUBS, span), f32),
+            pltpu.VMEM((everyone, trials, SUBS, span), f32),
+            pltpu.VMEM((GROUP, 2 * RADIX, wide), jnp.bfloat16),
+            pltpu.VMEM((GROUP, 2 * RADIX, wide), jnp.bfloat16),
+            pltpu.VMEM((GROUP, rows, LANES), f32),
+            *[pltpu.VMEM(c.shape, c.dtype) for c in consts],
+            dma((width // LANES, nb - 1)),
+            dma((width // LANES, nb - 1)),
+            dma((1 + groups, everyone - 1)),
+            dma((1 + groups, everyone - 1)),
+            dma((2,)),
+            dma((width // LANES,)),
+            dma((2,)),
+            dma((len(consts),)),
+            dma((GROUP,)),
+        ],
+        compiler_params=pltpu.CompilerParams(
+            collective_id=0, has_side_effects=True, vmem_limit_bytes=FUSED_LIMIT
+        ),
+        cost_estimate=pl.CostEstimate(
+            flops=6 * macs, bytes_accessed=3 * signal.size * 4, transcendentals=0
+        ),
+        name="fused",
+    )(picks, delays, u, view, *consts)
+
+
 def on_device(signal, tree_picks, tree_delays, template_bank, template_pick):
     band_count = lax.axis_size("band")
     time_count = lax.axis_size("tm")
@@ -324,6 +671,12 @@
     counts = [count for count in (trials - last, last) if count]
     zsel = template_pick.shape[2]
     taps = template_bank.shape[2]
+    cols = samples // RADIX
+    if width % (2 * cols) == 0 and trials % GROUP == 0:
+        u = reversed_taps(template_pick[0], template_bank)
+        consts = [jnp.asarray(c) for c in tables(samples, channels, width, taps)]
+        out = fused(signal, tree_picks, tree_delays, u, consts, zsel, taps, band_count, time_count)
+        return finish(out, trials, samples, zsel)
 
     band_high, band_low = bands(template_pick[0], template_bank)
 
@@ -375,8 +728,7 @@
         out, _ = spectra(
             arrived, band_high, band_low, consts, zsel, taps, trials, first, out
         )
-    out = out.reshape(trials, samples // 2 // LANES, zsel, LANES).transpose(0, 2, 1, 3)
-    return out.reshape(1, trials, zsel, samples // 2)
+    return finish(out, trials, samples, zsel)
 
 
 def solution(mesh):

time: 451 us -> 392 us (0.87)
  Pallas kernels: 109 us -> 380 us
  blocking collectives: 156 us -> 0 us
  waiting for transfers between devices: 144 us -> 0 us
  starting transfers between devices: 15.5 us -> 0 us
  local copies, waits for them, and re-layouts: 24.3 us -> 10.6 us
    pallas_call x8 -> x1, Pallas kernels: 109 us -> 380 us  [fused(): pl.pallas_call(functools.partial(fused_kernel, nb, nt, sections, trials,...]
    all_to_all x1 -> x0, blocking collectives: 156 us -> none  [on_device(): lax.all_to_all(piece, ('tm', 'band'), split_axis=0, concat_axis=0, tiled=...]
    all_to_all x3 -> x0, waiting for transfers between devices: 133 us -> none  [the longest x2 131 us: exchanged(): lax.all_to_all(value, 'band', split_axis=0, concat_axis=0, tiled=True)]
    all_to_all x3 -> x0, starting transfers between devices: 14.2 us -> none  [the longest x2 10.3 us: exchanged(): lax.all_to_all(value, 'band', split_axis=0, concat_axis=0, tiled=True)]
    ppermute x1 -> x0, waiting for transfers between devices: 11.3 us -> none  [shifted(): lax.ppermute(value, axis, [(source, source + steps) for source in range(f...]
    transpose x3 -> x0, local copies, waits for them, and re-layouts: 7.19 us -> none  [the longest x1 3.87 us: on_device(): x_b = after(after(folded[..., cut:].transpose(1, 0, 2, 3), x_a), band_low)]
    unnamed x18 -> x2, local copies, waits for them, and re-layouts: 13.1 us -> 7.43 us
  transfers between devices with their start and end apart: 4 -> 0, of which waited for: 4 -> 0; matrix products, arithmetic and copies ran while one was open for 2% -> 0% of each run, Pallas kernels for 16% -> 0%
where the time goes in v1:
time: 392 us
  Pallas kernels  380 us (97%)
  local copies, waits for them, and re-layouts  10.6 us (3%)
    pallas_call x1, Pallas kernels, fused(): pl.pallas_call(functools.partial(fused_kernel, nb, nt, sections, trials,...  380 us

profile of v1, /device:TPU:0, one launch (start us, length us, event | category | flops | bytes accessed | tf_op | source)
XLA Modules:
  0.0 391.6 jit_solution(4284024957964947280)
XLA Ops:
  0.0 0.1 pad.1.clone
  0.1 0.7 slice.6
  0.8 0.9 slice.7
  1.7 0.1 copy.18
  1.9 0.7 rev.3
  2.5 0.1 copy.13
  2.7 1.0 fusion
  3.7 0.7 copy.17.u_ref
  4.4 379.9 %fused.1 = f32[16,1024,128]{2,1,0:T(8,128)} custom-call(s32[2,8,256]{2,1,0:T(8,128)} %picks_ref.1, s32[8,256]{1,0:T(8,128)} %delay_ref.1, f32[16,4,256]{2,1,0:T(4,128)} %copy.17.u_ref, f32[8,4,64,1024]{3,2,1,0:T(8,128)} %bitcast.23, bf16[256,512]{1,0:T(8,128)(2,1)} %constant.14.clone.refs_0_, bf16[256,512]{1,0:T(8,128)(2,1)} %constant.15.clone.refs_1_, ...), custom_call_target="tpu_custom_call" | custom-call | flops 32212254720 | bytes 25165824 | tf_op jit(solution)/shard_map/fused/pallas_call | solution.py:621
  384.3 7.3 %copy.20 = f32[1,16,2,65536]{3,2,1,0:T(2,128)} copy(f32[1,16,2,65536]{3,2,1,0:T(2,128)} %bitcast.20) | data formatting | bytes 16777216
  (1 shorter events, 0.0 us)

commit v2 on v1

--- a/solution.py
+++ b/solution.py
@@ -18,8 +18,7 @@
 RADIX = 256
 LIMIT = 56 * 1024 * 1024
 FUSED_LIMIT = 62 * 1024 * 1024
-GROUP = 2
-AHEAD = 3
+AHEAD = 6
 MESH = pl.DeviceIdType.MESH
 
 
@@ -118,12 +117,11 @@
     return high, (value - high.astype(jnp.float32)).astype(jnp.bfloat16)
 
 
-def fill_bands(u, zsel, high_ref, low_ref):
+def fill_bands(row_of, zsel, high_ref, low_ref):
     for z in range(zsel):
         pair = []
         for part in range(2):
-            row = u[2 * z + part : 2 * z + part + 1, :]
-            wide = jnp.broadcast_to(row, (RADIX, RADIX))
+            wide = jnp.broadcast_to(row_of(z, part), (RADIX, RADIX))
             band = pltpu.roll(wide, 0, 1, stride=1, stride_axis=0)[:, :LANES]
             pair.append(split(band))
         at = 2 * z * LANES
@@ -138,7 +136,10 @@
 
 
 def bands_kernel(zsel, u_ref, high_ref, low_ref):
-    fill_bands(u_ref[0], zsel, high_ref.at[0], low_ref.at[0])
+    def row_of(z, part):
+        return u_ref[0, 2 * z + part : 2 * z + part + 1, :]
+
+    fill_bands(row_of, zsel, high_ref.at[0], low_ref.at[0])
 
 
 def reversed_taps(picks, template_bank):
@@ -340,22 +341,23 @@
 
 def fused_kernel(
     nb, nt, sections, trials, zsel, taps,
-    picks_ref, delay_ref, u_ref, sig_ref, *refs
+    picks_ref, delay_ref, wanted_ref, bank_ref, sig_ref, *refs
 ):
     const_refs, refs = refs[:6], refs[6:]
-    out_ref, refs = refs[0], refs[1:]
-    raw, refs = refs[0], refs[1:]
-    rim, buf_a, buf_b = refs[:3]
-    sent, got, refs = refs[3:5], refs[5:7], refs[7:]
-    band_high, band_low, power, refs = refs[0], refs[1], refs[2], refs[3:]
+    out_ref, last_x, last_bands, sent, refs = refs[0], refs[1:3], refs[3:5], refs[5:7], refs[7:]
+    raw, rim, buf_a, buf_b, stage, refs = *refs[:5], refs[5:]
+    got, refs = refs[:2], refs[2:]
+    band_high, band_low, power, bank, reverse, refs = *refs[:5], refs[5:]
     consts, refs = refs[:6], refs[6:]
-    one_send, one_recv, two_send, two_recv, rim_sems, own_one, own_two, const_sems, out_sems = refs
+    (
+        one_send, one_recv, two_send, two_recv, rim_sems, own_one, own_two, stage_sem,
+        load_sems, out_sems, last_sems,
+    ) = refs
 
     everyone = nb * nt
     rows, _, span = buf_a.shape
     span = span - LANES
     blocks = CH_DEV // SUBS
-    groups = trials // GROUP
     tiles = span // LANES
     early = range(tiles + 1)
     late = range(tiles + 1, 2 * tiles)
@@ -415,11 +417,24 @@
             first(i, d).start()
         first_own(i).start()
     loads = [
-        pltpu.make_async_copy(a, b, const_sems.at[i])
-        for i, (a, b) in enumerate(zip(const_refs, consts))
+        pltpu.make_async_copy(a, b, load_sems.at[i])
+        for i, (a, b) in enumerate(zip((bank_ref, *const_refs), (bank, *consts)))
     ]
     for load in loads:
         load.start()
+
+    loads[0].wait()
+    turn_row = lax.broadcasted_iota(jnp.int32, (taps, RADIX), 0)
+    turn_lane = lax.broadcasted_iota(jnp.int32, (taps, RADIX), 1)
+    turned_to = jnp.where((turn_row + turn_lane) % RADIX == 0, 1.0, 0.0).astype(jnp.float32)
+    for part in range(2):
+        reverse[part] = lax.dot_general(
+            bank[part],
+            turned_to,
+            (((0,), (0,)), ((), ())),
+            precision=lax.Precision.HIGHEST,
+            preferred_element_type=jnp.float32,
+        )
 
     lane = lax.broadcasted_iota(jnp.int32, (SUBS, LANES), 1)
     sub = lax.broadcasted_iota(jnp.int32, (SUBS, LANES), 0)
@@ -469,12 +484,18 @@
 
             @pl.loop(0, trials, unroll=trials)
             def _(i):
-                merge(src, sections - 1, start + i, sent[c].at[e], i, tiles)
-
-    def second(c, g, d):
+                merge(src, sections - 1, start + i, stage.at[e], i, tiles)
+
+        copy = pltpu.make_async_copy(stage, sent[c], stage_sem)
+        copy.start()
+        copy.wait()
+
+    def part_of(c, t):
+        return (pl.ds(t, 1), 1 + t) if c else (slice(None), 0)
+
+    def second(c, t, d):
         e = (me + d) % everyone
-        which = pl.ds(g * GROUP, GROUP) if c else slice(None)
-        at = 1 + g if c else 0
+        which, at = part_of(c, t)
         return pltpu.make_async_remote_copy(
             sent[c].at[e, which],
             got[c].at[me, which],
@@ -484,10 +505,9 @@
             device_id_type=MESH,
         )
 
-    def second_from(c, g, d):
+    def second_from(c, t, d):
         e = (me + everyone - d) % everyone
-        which = pl.ds(g * GROUP, GROUP) if c else slice(None)
-        at = 1 + g if c else 0
+        which, at = part_of(c, t)
         return pltpu.make_async_remote_copy(
             sent[c].at[e, which],
             got[c].at[e, which],
@@ -500,10 +520,16 @@
     def second_own(c):
         return pltpu.make_async_copy(sent[c].at[me], got[c].at[me], own_two.at[c])
 
-    def send_second(c, g):
+    def send_second(c, t):
         @pl.loop(1, everyone)
         def _(d):
-            second(c, g, d).start()
+            second(c, t, d).start()
+
+    def wait_second(c, t):
+        @pl.loop(1, everyone)
+        def _(d):
+            second_from(c, t, d).wait_recv()
+            second(c, t, d).wait_send()
 
     for i in early:
         first_wait(i)
@@ -536,8 +562,8 @@
 
     tree_part(1)
     second_own(1).start()
-    for g in range(min(AHEAD, groups)):
-        send_second(1, g)
+    for t in range(min(AHEAD, trials)):
+        send_second(1, t)
     for i in (*early, *late):
         for d in range(1, nb):
             first(i, d).wait_send()
@@ -546,57 +572,118 @@
     def _():
         rim_copy.wait_send()
 
-    for load in loads:
+    for load in loads[1:]:
         load.wait()
     second_own(0).wait()
     second_own(1).wait()
-
-    @pl.loop(1, everyone)
-    def _(d):
-        second_from(0, 0, d).wait_recv()
-        second(0, 0, d).wait_send()
-
-    cols = consts[2].shape[0]
+    wait_second(0, 0)
+
+    def bands_of(t, j):
+        def row(z, part):
+            return reverse[part, pl.ds(wanted_ref[z, t], 1), :]
+
+        fill_bands(row, zsel, band_high.at[j], band_low.at[j])
 
     def out_copy(t, j):
         return pltpu.make_async_copy(power.at[j], out_ref.at[t], out_sems.at[j])
 
-    @pl.loop(0, groups)
+    def spectra_of(t, j):
+        x = assemble([got[c][:, t] for c in range(2)], consts)
+
+        def store(where, value):
+            power[j, where, :] = value
+
+        powers_of(x, band_high[j], band_low[j], consts, zsel, taps // 2, store)
+        out_copy(t, j).start()
+
+    @pl.loop(0, trials // 2 - 1)
     def _(g):
-        for j in range(GROUP):
-            fill_bands(u_ref[g * GROUP + j], zsel, band_high.at[j], band_low.at[j])
-
-        @pl.loop(1, everyone)
-        def _(d):
-            second_from(1, g, d).wait_recv()
-            second(1, g, d).wait_send()
-
-        @pl.when(g + AHEAD < groups)
-        def _():
-            send_second(1, g + AHEAD)
-
-        for j in range(GROUP):
-            t = g * GROUP + j
-            parts = [got[c][:, t].reshape(everyone * SUBS, span) for c in range(2)]
-            x = jnp.concatenate(
-                [part[:, i : i + cols] for part in parts for i in range(0, span, cols)], axis=0
-            )
+        for j in range(2):
+            bands_of(2 * g + j, j)
+        for j in range(2):
+            t = 2 * g + j
+            wait_second(1, t)
+
+            @pl.when(t + AHEAD < trials)
+            def _(t=t):
+                send_second(1, t + AHEAD)
 
             @pl.when(g > 0)
             def _(j=j, t=t):
-                out_copy(t - GROUP, j).wait()
-
-            def store(where, value, j=j):
-                power[j, where, :] = value
-
-            powers_of(x, band_high[j], band_low[j], consts, zsel, taps // 2, store)
-            out_copy(t, j).start()
-
-    for j in range(GROUP):
-        out_copy(trials - GROUP + j, j).wait()
-
-
-def fused(signal, picks, delays, u, consts, zsel, taps, nb, nt):
+                out_copy(t - 2, j).wait()
+
+            spectra_of(t, j)
+
+    last = trials - 1
+    for j in range(2):
+        bands_of(last - 1 + j, j)
+    band_copies = [
+        pltpu.make_async_copy(source.at[1], target, last_sems.at[2 + i])
+        for i, (source, target) in enumerate(zip((band_high, band_low), last_bands))
+    ]
+    for copy in band_copies:
+        copy.start()
+    wait_second(1, last - 1)
+    out_copy(last - 3, 0).wait()
+    spectra_of(last - 1, 0)
+    wait_second(1, last)
+    x_copies = [
+        pltpu.make_async_copy(got[c].at[:, last], last_x[c], last_sems.at[c]) for c in range(2)
+    ]
+    for copy in x_copies:
+        copy.start()
+    out_copy(last - 2, 1).wait()
+    out_copy(last - 1, 0).wait()
+    for copy in (*band_copies, *x_copies):
+        copy.wait()
+
+
+def assemble(parts, consts):
+    cols = consts[2].shape[0]
+    parts = [part.reshape(-1, part.shape[-1]) for part in parts]
+    return jnp.concatenate(
+        [part[:, i : i + cols] for part in parts for i in range(0, part.shape[1], cols)], axis=0
+    )
+
+
+def last_kernel(zsel, half_taps, *refs):
+    done_ref, inputs, out_ref, refs = refs[0], refs[1:11], refs[11], refs[12:]
+    held, moved, power, sems, move_sems = refs[:10], *refs[10:]
+    loads = [
+        pltpu.make_async_copy(a, b, sems.at[i]) for i, (a, b) in enumerate(zip(inputs, held))
+    ]
+    for load in loads:
+        load.start()
+    count = done_ref.shape[0]
+    fetch = [
+        pltpu.make_async_copy(done_ref.at[t], moved.at[t], move_sems.at[0, t])
+        for t in range(count)
+    ]
+    store_back = [
+        pltpu.make_async_copy(moved.at[t], out_ref.at[t], move_sems.at[1, t])
+        for t in range(count)
+    ]
+    for move in fetch:
+        move.start()
+    for load in loads:
+        load.wait()
+    for move, back in zip(fetch, store_back):
+        move.wait()
+        back.start()
+    x = assemble([held[0][...], held[1][...]], held[4:])
+
+    def store(where, value):
+        power[where, :] = value
+
+    powers_of(x, held[2][...], held[3][...], held[4:], zsel, half_taps, store)
+    final = pltpu.make_async_copy(power, out_ref.at[count], sems.at[len(loads)])
+    final.start()
+    for back in store_back:
+        back.wait()
+    final.wait()
+
+
+def fused(signal, picks, delays, template_bank, wanted, consts, zsel, taps, nb, nt):
     sections = picks.shape[1]
     channels = CH_DEV * nb
     everyone = nb * nt
@@ -608,52 +695,77 @@
     cols = consts[2].shape[0]
     outs = cols // 2
     rows = 2 * outs * zsel
-    groups = trials // GROUP
     wide = 2 * zsel * LANES
     view = signal.reshape(blocks, SUBS, nb * SUBS, width).transpose(0, 2, 1, 3)
     view = view.reshape(blocks, nb, SUBS * SUBS, width)
+    bank = template_bank.transpose(0, 2, 1)
     smem = pl.BlockSpec(memory_space=pltpu.SMEM)
-    vmem = pl.BlockSpec(memory_space=pltpu.VMEM)
     anywhere = pl.BlockSpec(memory_space=pl.ANY)
     dma = pltpu.SemaphoreType.DMA
-    f32 = jnp.float32
-    macs = trials * (cols * RADIX * 2 * RADIX + outs * 2 * cols * 2 * RADIX + 2 * outs * 4 * RADIX * RADIX)
-    return pl.pallas_call(
+    f32, bf16 = jnp.float32, jnp.bfloat16
+    macs = cols * RADIX * 2 * RADIX + outs * 2 * cols * 2 * RADIX + 2 * outs * 4 * RADIX * RADIX
+    arrays = jax.ShapeDtypeStruct
+    exchanged = (everyone, trials, SUBS, span)
+    last = [arrays((everyone, SUBS, span), f32)] * 2 + [arrays((2 * RADIX, wide), bf16)] * 2
+    scratch_consts = [pltpu.VMEM(c.shape, c.dtype) for c in consts]
+    done, *rest = pl.pallas_call(
         functools.partial(fused_kernel, nb, nt, sections, trials, zsel, taps),
-        out_shape=jax.ShapeDtypeStruct((trials, rows, LANES), f32),
-        in_specs=[smem, smem, vmem] + [anywhere] * 7,
-        out_specs=anywhere,
+        out_shape=[arrays((trials - 1, rows, LANES), f32)] + last + [arrays(exchanged, f32)] * 2,
+        in_specs=[smem] * 3 + [anywhere] * 8,
+        out_specs=[anywhere] * 7,
         scratch_shapes=[
             pltpu.VMEM((nb * blocks, width // LANES, SUBS * SUBS, LANES), f32),
             pltpu.VMEM((nb * blocks, SUBS, LANES), f32),
             pltpu.VMEM((channels, SUBS, span + LANES), f32),
             pltpu.VMEM((channels, SUBS, span + LANES), f32),
-            pltpu.VMEM((everyone, trials, SUBS, span), f32),
-            pltpu.VMEM((everyone, trials, SUBS, span), f32),
-            pltpu.VMEM((everyone, trials, SUBS, span), f32),
-            pltpu.VMEM((everyone, trials, SUBS, span), f32),
-            pltpu.VMEM((GROUP, 2 * RADIX, wide), jnp.bfloat16),
-            pltpu.VMEM((GROUP, 2 * RADIX, wide), jnp.bfloat16),
-            pltpu.VMEM((GROUP, rows, LANES), f32),
-            *[pltpu.VMEM(c.shape, c.dtype) for c in consts],
+            pltpu.VMEM(exchanged, f32),
+            pltpu.VMEM(exchanged, f32),
+            pltpu.VMEM(exchanged, f32),
+            pltpu.VMEM((2, 2 * RADIX, wide), bf16),
+            pltpu.VMEM((2, 2 * RADIX, wide), bf16),
+            pltpu.VMEM((2, rows, LANES), f32),
+            pltpu.VMEM(bank.shape, f32),
+            pltpu.VMEM(template_bank.shape[:2] + (RADIX,), f32),
+            *scratch_consts,
             dma((width // LANES, nb - 1)),
             dma((width // LANES, nb - 1)),
-            dma((1 + groups, everyone - 1)),
-            dma((1 + groups, everyone - 1)),
+            dma((1 + trials, everyone - 1)),
+            dma((1 + trials, everyone - 1)),
             dma((2,)),
             dma((width // LANES,)),
             dma((2,)),
-            dma((len(consts),)),
-            dma((GROUP,)),
+            dma,
+            dma((1 + len(consts),)),
+            dma((2,)),
+            dma((4,)),
         ],
         compiler_params=pltpu.CompilerParams(
             collective_id=0, has_side_effects=True, vmem_limit_bytes=FUSED_LIMIT
         ),
         cost_estimate=pl.CostEstimate(
+            flops=6 * trials * macs, bytes_accessed=3 * signal.size * 4, transcendentals=0
+        ),
+        name="fused",
+    )(picks, delays, wanted.T, bank, view, *consts)
+    return pl.pallas_call(
+        functools.partial(last_kernel, zsel, taps // 2),
+        out_shape=arrays((trials, rows, LANES), f32),
+        in_specs=[anywhere] * 11,
+        out_specs=anywhere,
+        scratch_shapes=[
+            *[pltpu.VMEM(a.shape, a.dtype) for a in last],
+            *scratch_consts,
+            pltpu.VMEM((trials - 1, rows, LANES), f32),
+            pltpu.VMEM((rows, LANES), f32),
+            dma((11,)),
+            dma((2, trials - 1)),
+        ],
+        compiler_params=pltpu.CompilerParams(vmem_limit_bytes=LIMIT),
+        cost_estimate=pl.CostEstimate(
             flops=6 * macs, bytes_accessed=3 * signal.size * 4, transcendentals=0
         ),
-        name="fused",
-    )(picks, delays, u, view, *consts)
+        name="last",
+    )(done, *rest[:4], *consts)
 
 
 def on_device(signal, tree_picks, tree_delays, template_bank, template_pick):
@@ -672,10 +784,12 @@
     zsel = template_pick.shape[2]
     taps = template_bank.shape[2]
     cols = samples // RADIX
-    if width % (2 * cols) == 0 and trials % GROUP == 0:
-        u = reversed_taps(template_pick[0], template_bank)
+    if width % (2 * cols) == 0 and trials % 2 == 0 and trials >= 4:
         consts = [jnp.asarray(c) for c in tables(samples, channels, width, taps)]
-        out = fused(signal, tree_picks, tree_delays, u, consts, zsel, taps, band_count, time_count)
+        out = fused(
+            signal, tree_picks, tree_delays, template_bank, template_pick[0], consts, zsel, taps,
+            band_count, time_count,
+        )
         return finish(out, trials, samples, zsel)
 
     band_high, band_low = bands(template_pick[0], template_bank)

time: 392 us -> 386 us (0.985)
  local copies, waits for them, and re-layouts: 10.6 us -> 0 us
  Pallas kernels: 380 us -> 386 us
    pallas_call x0 -> x1, Pallas kernels: none -> 8.06 us  [fused(): pl.pallas_call(functools.partial(last_kernel, zsel, taps // 2), out_shape...]
    unnamed x2 -> x0, local copies, waits for them, and re-layouts: 7.43 us -> none
where the time goes in v2:
time: 386 us
  Pallas kernels  386 us (100%)
    pallas_call x1, Pallas kernels, fused(): pl.pallas_call(functools.partial(fused_kernel, nb, nt, sections, trials,...  378 us
    pallas_call x1, Pallas kernels, fused(): pl.pallas_call(functools.partial(last_kernel, zsel, taps // 2), out_shape...  8.06 us

profile of v2, /device:TPU:0, one launch (start us, length us, event | category | flops | bytes accessed | tf_op | source)
XLA Modules:
  0.0 385.9 jit_solution(4506223603565794856)
XLA Ops:
  0.0 377.6 %fused.1 = (f32[15,1024,128]{2,1,0:T(8,128)}, f32[16,8,512]{2,1,0:T(8,128)}, f32[16,8,512]{2,1,0:T(8,128)}, bf16[512,512]{1,0:T(8,128)(2,1)}, bf16[512,512]{1,0:...) custom-call(s32[2,8,256]{2,1,0:T(8,128)} %picks_ref.1, s32[8,256]{1,0:T(8,128)} %delay_ref.1, ...), custom_call_target="tpu_custom_call" | custom-call | flops 32212254720 | bytes 25165824 | tf_op jit(solution)/shard_map/fused/pallas_call | solution.py:711
  377.6 8.1 %last.1 = f32[16,1024,128]{2,1,0:T(8,128)} custom-call(f32[15,1024,128]{2,1,0:T(8,128)} %get-tuple-element.10.refs_0_, f32[16,8,512]{2,1,0:T(8,128)} %get-tuple-element.11.refs_1_, f32[16,8,512]{2,1,0:T(8,128)} %get-tuple-element.12.refs_2_, bf16[512,512]{1,0:T(8,128)(2,1)} %get-tuple-element.13.refs_3_, bf16[512,512]{1,0:T(8,128)(2,1)} %get-tuple-element.14.refs_4_, ...), custom_call_target="tpu_custom_call" | custom-call | flops 2013265920 | bytes 25165824 | tf_op jit(solution)/shard_map/last/pallas_call | solution.py:750

commit v3 on v2

--- a/solution.py
+++ b/solution.py
@@ -218,12 +218,14 @@
     return dot(a_high, b_high) + (dot(a_high, b_low) + dot(a_low, b_high))
 
 
-def powers_of(x, band_high, band_low, consts, zsel, half_taps, store):
+def powers_of(x, band_high, band_low, consts, zsel, half_taps, store, between=()):
     fh, fl, tc, ts, sh, sl = consts
     cols = tc.shape[0]
     outs = cols // 2
     x_high, x_low = split(x.T)
     first = dot3(x_high, x_low, fh[...], fl[...])
+    if between:
+        between[0]()
     re, im = first[:, :RADIX], first[:, RADIX:]
     mid_re = re * tc[...] + im * ts[...]
     mid_im = im * tc[...] - re * ts[...]
@@ -236,6 +238,8 @@
         )
 
     spec = dot3(sh[...], sl[...], block(re_high, im_high), block(re_low, im_low))
+    if between:
+        between[1]()
     row = lax.broadcasted_iota(jnp.int32, (outs, RADIX), 0)
     lane = lax.broadcasted_iota(jnp.int32, (outs, RADIX), 1)
     even, odd = [], []
@@ -341,7 +345,7 @@
 
 def fused_kernel(
     nb, nt, sections, trials, zsel, taps,
-    picks_ref, delay_ref, wanted_ref, bank_ref, sig_ref, *refs
+    picks_hbm, delay_hbm, wanted_hbm, bank_ref, sig_ref, *refs
 ):
     const_refs, refs = refs[:6], refs[6:]
     out_ref, last_x, last_bands, sent, refs = refs[0], refs[1:3], refs[3:5], refs[5:7], refs[7:]
@@ -349,9 +353,9 @@
     got, refs = refs[:2], refs[2:]
     band_high, band_low, power, bank, reverse, refs = *refs[:5], refs[5:]
     consts, refs = refs[:6], refs[6:]
+    picks_ref, delay_ref, wanted_ref, refs = *refs[:3], refs[3:]
     (
-        one_send, one_recv, two_send, two_recv, rim_sems, own_one, own_two, stage_sem,
-        load_sems, out_sems, last_sems,
+        one_send, one_recv, two_send, two_recv, rim_sems, stage_sem, load_sems, out_sems, last_sems,
     ) = refs
 
     everyone = nb * nt
@@ -380,36 +384,26 @@
     def slab(i, k):
         return sig_ref.at[:, k, :, pl.ds(i * LANES, LANES)]
 
+    def landed(ref, sem):
+        pltpu.make_async_copy(ref, ref, sem).wait()
+
     def first(i, d):
         return pltpu.make_async_remote_copy(
             slab(i, (mb + d) % nb),
             raw.at[pl.ds(mb * blocks, blocks), i],
-            one_send.at[i, d - 1],
-            one_recv.at[i, d - 1],
+            one_send,
+            one_recv.at[i],
             device_id={"band": (mb + d) % nb},
             device_id_type=MESH,
         )
 
-    def first_from(i, d):
-        source = (mb + nb - d) % nb
-        return pltpu.make_async_remote_copy(
-            slab(i, mb),
-            raw.at[pl.ds(source * blocks, blocks), i],
-            one_send.at[i, d - 1],
-            one_recv.at[i, d - 1],
-            device_id={"band": source},
-            device_id_type=MESH,
-        )
-
     def first_own(i):
         return pltpu.make_async_copy(
-            slab(i, mb), raw.at[pl.ds(mb * blocks, blocks), i], own_one.at[i]
+            slab(i, mb), raw.at[pl.ds(mb * blocks, blocks), i], one_recv.at[i]
         )
 
     def first_wait(i):
-        for d in range(1, nb):
-            first_from(i, d).wait_recv()
-        first_own(i).wait()
+        landed(raw.at[:, i], one_recv.at[i])
 
     apart = sorted(range(1, nb), key=lambda d: -min(d, nb - d))
     for i in (*early, *late):
@@ -418,12 +412,16 @@
         first_own(i).start()
     loads = [
         pltpu.make_async_copy(a, b, load_sems.at[i])
-        for i, (a, b) in enumerate(zip((bank_ref, *const_refs), (bank, *consts)))
+        for i, (a, b) in enumerate(zip(
+            (bank_ref, picks_hbm, delay_hbm, wanted_hbm, *const_refs),
+            (bank, picks_ref, delay_ref, wanted_ref, *consts),
+        ))
     ]
     for load in loads:
         load.start()
 
-    loads[0].wait()
+    for load in loads[:4]:
+        load.wait()
     turn_row = lax.broadcasted_iota(jnp.int32, (taps, RADIX), 0)
     turn_lane = lax.broadcasted_iota(jnp.int32, (taps, RADIX), 1)
     turned_to = jnp.where((turn_row + turn_lane) % RADIX == 0, 1.0, 0.0).astype(jnp.float32)
@@ -499,37 +497,25 @@
         return pltpu.make_async_remote_copy(
             sent[c].at[e, which],
             got[c].at[me, which],
-            two_send.at[at, d - 1],
-            two_recv.at[at, d - 1],
+            two_send.at[c],
+            two_recv.at[at],
             device_id=device(e),
             device_id_type=MESH,
         )
-
-    def second_from(c, t, d):
-        e = (me + everyone - d) % everyone
-        which, at = part_of(c, t)
-        return pltpu.make_async_remote_copy(
-            sent[c].at[e, which],
-            got[c].at[e, which],
-            two_send.at[at, d - 1],
-            two_recv.at[at, d - 1],
-            device_id=device(e),
-            device_id_type=MESH,
-        )
-
-    def second_own(c):
-        return pltpu.make_async_copy(sent[c].at[me], got[c].at[me], own_two.at[c])
 
     def send_second(c, t):
         @pl.loop(1, everyone)
         def _(d):
             second(c, t, d).start()
 
+        which, at = part_of(c, t)
+        pltpu.make_async_copy(
+            sent[c].at[me, which], got[c].at[me, which], two_recv.at[at]
+        ).start()
+
     def wait_second(c, t):
-        @pl.loop(1, everyone)
-        def _(d):
-            second_from(c, t, d).wait_recv()
-            second(c, t, d).wait_send()
+        which, at = part_of(c, t)
+        landed(got[c].at[:, which], two_recv.at[at])
 
     for i in early:
         first_wait(i)
@@ -552,7 +538,6 @@
 
     tree_part(0)
     send_second(0, 0)
-    second_own(0).start()
     for i in late:
         first_wait(i)
 
@@ -561,21 +546,16 @@
         rim_copy.wait_recv()
 
     tree_part(1)
-    second_own(1).start()
     for t in range(min(AHEAD, trials)):
         send_second(1, t)
-    for i in (*early, *late):
-        for d in range(1, nb):
-            first(i, d).wait_send()
+    landed(raw.at[pl.ds(0, (nb - 1) * blocks)], one_send)
 
     @pl.when(me > 0)
     def _():
         rim_copy.wait_send()
 
-    for load in loads[1:]:
+    for load in loads[4:]:
         load.wait()
-    second_own(0).wait()
-    second_own(1).wait()
     wait_second(0, 0)
 
     def bands_of(t, j):
@@ -636,6 +616,8 @@
     out_copy(last - 1, 0).wait()
     for copy in (*band_copies, *x_copies):
         copy.wait()
+    for c in range(2):
+        landed(sent[c].at[pl.ds(0, everyone - 1)], two_send.at[c])
 
 
 def assemble(parts, consts):
@@ -667,15 +649,19 @@
         move.start()
     for load in loads:
         load.wait()
-    for move, back in zip(fetch, store_back):
-        move.wait()
-        back.start()
+
+    def move_on(begin, end):
+        for move, back in zip(fetch[begin:end], store_back[begin:end]):
+            move.wait()
+            back.start()
+
+    between = (lambda: move_on(0, count // 2), lambda: move_on(count // 2, count))
     x = assemble([held[0][...], held[1][...]], held[4:])
 
     def store(where, value):
         power[where, :] = value
 
-    powers_of(x, held[2][...], held[3][...], held[4:], zsel, half_taps, store)
+    powers_of(x, held[2][...], held[3][...], held[4:], zsel, half_taps, store, between)
     final = pltpu.make_async_copy(power, out_ref.at[count], sems.at[len(loads)])
     final.start()
     for back in store_back:
@@ -699,7 +685,6 @@
     view = signal.reshape(blocks, SUBS, nb * SUBS, width).transpose(0, 2, 1, 3)
     view = view.reshape(blocks, nb, SUBS * SUBS, width)
     bank = template_bank.transpose(0, 2, 1)
-    smem = pl.BlockSpec(memory_space=pltpu.SMEM)
     anywhere = pl.BlockSpec(memory_space=pl.ANY)
     dma = pltpu.SemaphoreType.DMA
     f32, bf16 = jnp.float32, jnp.bfloat16
@@ -711,7 +696,7 @@
     done, *rest = pl.pallas_call(
         functools.partial(fused_kernel, nb, nt, sections, trials, zsel, taps),
         out_shape=[arrays((trials - 1, rows, LANES), f32)] + last + [arrays(exchanged, f32)] * 2,
-        in_specs=[smem] * 3 + [anywhere] * 8,
+        in_specs=[anywhere] * 11,
         out_specs=[anywhere] * 7,
         scratch_shapes=[
             pltpu.VMEM((nb * blocks, width // LANES, SUBS * SUBS, LANES), f32),
@@ -727,15 +712,14 @@
             pltpu.VMEM(bank.shape, f32),
             pltpu.VMEM(template_bank.shape[:2] + (RADIX,), f32),
             *scratch_consts,
-            dma((width // LANES, nb - 1)),
-            dma((width // LANES, nb - 1)),
-            dma((1 + trials, everyone - 1)),
-            dma((1 + trials, everyone - 1)),
-            dma((2,)),
+            *[pltpu.SMEM(a.shape, jnp.int32) for a in (picks, delays, wanted.T)],
+            dma,
             dma((width // LANES,)),
             dma((2,)),
+            dma((1 + trials,)),
+            dma((2,)),
             dma,
-            dma((1 + len(consts),)),
+            dma((4 + len(consts),)),
             dma((2,)),
             dma((4,)),
         ],

time: 386 us -> 380 us (0.984)
  Pallas kernels: 386 us -> 380 us
    pallas_call x1, Pallas kernels: 378 us -> 371 us  [fused(): pl.pallas_call(functools.partial(fused_kernel, nb, nt, sections, trials,...]
where the time goes in v3:
time: 380 us
  Pallas kernels  380 us (100%)
    pallas_call x1, Pallas kernels, fused(): pl.pallas_call(functools.partial(fused_kernel, nb, nt, sections, trials,...  371 us
    pallas_call x1, Pallas kernels, fused(): pl.pallas_call(functools.partial(last_kernel, zsel, taps // 2), out_shape...  8.6 us

profile of v3, /device:TPU:0, one launch (start us, length us, event | category | flops | bytes accessed | tf_op | source)
XLA Modules:
  0.0 379.9 jit_solution(9469596602388544042)
XLA Ops:
  0.0 371.3 %fused.1 = (f32[15,1024,128]{2,1,0:T(8,128)}, f32[16,8,512]{2,1,0:T(8,128)}, f32[16,8,512]{2,1,0:T(8,128)}, bf16[512,512]{1,0:T(8,128)(2,1)}, bf16[512,512]{1,0:...) custom-call(s32[2,8,256]{2,1,0:T(8,128)} %picks_hbm.1, s32[8,256]{1,0:T(8,128)} %delay_hbm.1, ...), custom_call_target="tpu_custom_call" | custom-call | flops 32212254720 | bytes 25165824 | tf_op jit(solution)/shard_map/fused/pallas_call | solution.py:696
  371.3 8.6 %last.1 = f32[16,1024,128]{2,1,0:T(8,128)} custom-call(f32[15,1024,128]{2,1,0:T(8,128)} %get-tuple-element.10.refs_0_, f32[16,8,512]{2,1,0:T(8,128)} %get-tuple-element.11.refs_1_, f32[16,8,512]{2,1,0:T(8,128)} %get-tuple-element.12.refs_2_, bf16[512,512]{1,0:T(8,128)(2,1)} %get-tuple-element.13.refs_3_, bf16[512,512]{1,0:T(8,128)(2,1)} %get-tuple-element.14.refs_4_, ...), custom_call_target="tpu_custom_call" | custom-call | flops 2013265920 | bytes 25165824 | tf_op jit(solution)/shard_map/last/pallas_call | solution.py:734

commit v4 on v3

--- a/solution.py
+++ b/solution.py
@@ -17,7 +17,8 @@
 SUBS = 8
 RADIX = 256
 LIMIT = 56 * 1024 * 1024
-FUSED_LIMIT = 62 * 1024 * 1024
+FUSED_LIMIT = 48 * 1024 * 1024
+LAST_LIMIT = 14 * 1024 * 1024
 AHEAD = 6
 MESH = pl.DeviceIdType.MESH
 
@@ -218,14 +219,12 @@
     return dot(a_high, b_high) + (dot(a_high, b_low) + dot(a_low, b_high))
 
 
-def powers_of(x, band_high, band_low, consts, zsel, half_taps, store, between=()):
+def powers_of(x, band_high, band_low, consts, zsel, half_taps, store):
     fh, fl, tc, ts, sh, sl = consts
     cols = tc.shape[0]
     outs = cols // 2
     x_high, x_low = split(x.T)
     first = dot3(x_high, x_low, fh[...], fl[...])
-    if between:
-        between[0]()
     re, im = first[:, :RADIX], first[:, RADIX:]
     mid_re = re * tc[...] + im * ts[...]
     mid_im = im * tc[...] - re * ts[...]
@@ -238,8 +237,6 @@
         )
 
     spec = dot3(sh[...], sl[...], block(re_high, im_high), block(re_low, im_low))
-    if between:
-        between[1]()
     row = lax.broadcasted_iota(jnp.int32, (outs, RADIX), 0)
     lane = lax.broadcasted_iota(jnp.int32, (outs, RADIX), 1)
     even, odd = [], []
@@ -348,14 +345,14 @@
     picks_hbm, delay_hbm, wanted_hbm, bank_ref, sig_ref, *refs
 ):
     const_refs, refs = refs[:6], refs[6:]
-    out_ref, last_x, last_bands, sent, refs = refs[0], refs[1:3], refs[3:5], refs[5:7], refs[7:]
+    power, last_x, band_high, band_low, refs = refs[0], refs[1:3], refs[3], refs[4], refs[5:]
+    consts, sent, refs = refs[:6], refs[6:8], refs[8:]
     raw, rim, buf_a, buf_b, stage, refs = *refs[:5], refs[5:]
     got, refs = refs[:2], refs[2:]
-    band_high, band_low, power, bank, reverse, refs = *refs[:5], refs[5:]
-    consts, refs = refs[:6], refs[6:]
+    bank, reverse, refs = *refs[:2], refs[2:]
     picks_ref, delay_ref, wanted_ref, refs = *refs[:3], refs[3:]
     (
-        one_send, one_recv, two_send, two_recv, rim_sems, stage_sem, load_sems, out_sems, last_sems,
+        one_send, one_recv, two_send, two_recv, rim_sems, stage_sem, load_sems, last_sems,
     ) = refs
 
     everyone = nb * nt
@@ -558,63 +555,37 @@
         load.wait()
     wait_second(0, 0)
 
-    def bands_of(t, j):
+    def bands_of(t):
         def row(z, part):
             return reverse[part, pl.ds(wanted_ref[z, t], 1), :]
 
-        fill_bands(row, zsel, band_high.at[j], band_low.at[j])
-
-    def out_copy(t, j):
-        return pltpu.make_async_copy(power.at[j], out_ref.at[t], out_sems.at[j])
-
-    def spectra_of(t, j):
+        fill_bands(row, zsel, band_high, band_low)
+
+    last = trials - 1
+
+    @pl.loop(0, last)
+    def _(t):
+        bands_of(t)
+        wait_second(1, t)
+
+        @pl.when(t + AHEAD < trials)
+        def _():
+            send_second(1, t + AHEAD)
+
+        def store(where, value):
+            power[t, where, :] = value
+
         x = assemble([got[c][:, t] for c in range(2)], consts)
-
-        def store(where, value):
-            power[j, where, :] = value
-
-        powers_of(x, band_high[j], band_low[j], consts, zsel, taps // 2, store)
-        out_copy(t, j).start()
-
-    @pl.loop(0, trials // 2 - 1)
-    def _(g):
-        for j in range(2):
-            bands_of(2 * g + j, j)
-        for j in range(2):
-            t = 2 * g + j
-            wait_second(1, t)
-
-            @pl.when(t + AHEAD < trials)
-            def _(t=t):
-                send_second(1, t + AHEAD)
-
-            @pl.when(g > 0)
-            def _(j=j, t=t):
-                out_copy(t - 2, j).wait()
-
-            spectra_of(t, j)
-
-    last = trials - 1
-    for j in range(2):
-        bands_of(last - 1 + j, j)
-    band_copies = [
-        pltpu.make_async_copy(source.at[1], target, last_sems.at[2 + i])
-        for i, (source, target) in enumerate(zip((band_high, band_low), last_bands))
-    ]
-    for copy in band_copies:
-        copy.start()
-    wait_second(1, last - 1)
-    out_copy(last - 3, 0).wait()
-    spectra_of(last - 1, 0)
+        powers_of(x, band_high[...], band_low[...], consts, zsel, taps // 2, store)
+
+    bands_of(last)
     wait_second(1, last)
     x_copies = [
         pltpu.make_async_copy(got[c].at[:, last], last_x[c], last_sems.at[c]) for c in range(2)
     ]
     for copy in x_copies:
         copy.start()
-    out_copy(last - 2, 1).wait()
-    out_copy(last - 1, 0).wait()
-    for copy in (*band_copies, *x_copies):
+    for copy in x_copies:
         copy.wait()
     for c in range(2):
         landed(sent[c].at[pl.ds(0, everyone - 1)], two_send.at[c])
@@ -629,43 +600,20 @@
 
 
 def last_kernel(zsel, half_taps, *refs):
-    done_ref, inputs, out_ref, refs = refs[0], refs[1:11], refs[11], refs[12:]
-    held, moved, power, sems, move_sems = refs[:10], *refs[10:]
-    loads = [
-        pltpu.make_async_copy(a, b, sems.at[i]) for i, (a, b) in enumerate(zip(inputs, held))
-    ]
-    for load in loads:
-        load.start()
+    done_ref, early_x, late_x, band_high, band_low = refs[:5]
+    consts, out_ref, power, move_sem, sem = refs[5:11], *refs[11:]
     count = done_ref.shape[0]
-    fetch = [
-        pltpu.make_async_copy(done_ref.at[t], moved.at[t], move_sems.at[0, t])
-        for t in range(count)
-    ]
-    store_back = [
-        pltpu.make_async_copy(moved.at[t], out_ref.at[t], move_sems.at[1, t])
-        for t in range(count)
-    ]
-    for move in fetch:
-        move.start()
-    for load in loads:
-        load.wait()
-
-    def move_on(begin, end):
-        for move, back in zip(fetch[begin:end], store_back[begin:end]):
-            move.wait()
-            back.start()
-
-    between = (lambda: move_on(0, count // 2), lambda: move_on(count // 2, count))
-    x = assemble([held[0][...], held[1][...]], held[4:])
+    move = pltpu.make_async_copy(done_ref, out_ref.at[pl.ds(0, count)], move_sem)
+    move.start()
+    x = assemble([early_x[...], late_x[...]], consts)
 
     def store(where, value):
         power[where, :] = value
 
-    powers_of(x, held[2][...], held[3][...], held[4:], zsel, half_taps, store, between)
-    final = pltpu.make_async_copy(power, out_ref.at[count], sems.at[len(loads)])
+    powers_of(x, band_high[...], band_low[...], consts, zsel, half_taps, store)
+    final = pltpu.make_async_copy(power, out_ref.at[count], sem)
     final.start()
-    for back in store_back:
-        back.wait()
+    move.wait()
     final.wait()
 
 
@@ -689,15 +637,19 @@
     dma = pltpu.SemaphoreType.DMA
     f32, bf16 = jnp.float32, jnp.bfloat16
     macs = cols * RADIX * 2 * RADIX + outs * 2 * cols * 2 * RADIX + 2 * outs * 4 * RADIX * RADIX
-    arrays = jax.ShapeDtypeStruct
     exchanged = (everyone, trials, SUBS, span)
-    last = [arrays((everyone, SUBS, span), f32)] * 2 + [arrays((2 * RADIX, wide), bf16)] * 2
-    scratch_consts = [pltpu.VMEM(c.shape, c.dtype) for c in consts]
-    done, *rest = pl.pallas_call(
+    kept = [
+        pltpu.VMEM((trials - 1, rows, LANES), f32),
+        *[pltpu.VMEM((everyone, SUBS, span), f32)] * 2,
+        *[pltpu.VMEM((2 * RADIX, wide), bf16)] * 2,
+        *[pltpu.VMEM(c.shape, c.dtype) for c in consts],
+    ]
+    vmem = pl.BlockSpec(memory_space=pltpu.VMEM)
+    *handed, _, _ = pl.pallas_call(
         functools.partial(fused_kernel, nb, nt, sections, trials, zsel, taps),
-        out_shape=[arrays((trials - 1, rows, LANES), f32)] + last + [arrays(exchanged, f32)] * 2,
+        out_shape=kept + [jax.ShapeDtypeStruct(exchanged, f32)] * 2,
         in_specs=[anywhere] * 11,
-        out_specs=[anywhere] * 7,
+        out_specs=[vmem] * len(kept) + [anywhere] * 2,
         scratch_shapes=[
             pltpu.VMEM((nb * blocks, width // LANES, SUBS * SUBS, LANES), f32),
             pltpu.VMEM((nb * blocks, SUBS, LANES), f32),
@@ -706,12 +658,8 @@
             pltpu.VMEM(exchanged, f32),
             pltpu.VMEM(exchanged, f32),
             pltpu.VMEM(exchanged, f32),
-            pltpu.VMEM((2, 2 * RADIX, wide), bf16),
-            pltpu.VMEM((2, 2 * RADIX, wide), bf16),
-            pltpu.VMEM((2, rows, LANES), f32),
             pltpu.VMEM(bank.shape, f32),
             pltpu.VMEM(template_bank.shape[:2] + (RADIX,), f32),
-            *scratch_consts,
             *[pltpu.SMEM(a.shape, jnp.int32) for a in (picks, delays, wanted.T)],
             dma,
             dma((width // LANES,)),
@@ -721,7 +669,6 @@
             dma,
             dma((4 + len(consts),)),
             dma((2,)),
-            dma((4,)),
         ],
         compiler_params=pltpu.CompilerParams(
             collective_id=0, has_side_effects=True, vmem_limit_bytes=FUSED_LIMIT
@@ -733,23 +680,16 @@
     )(picks, delays, wanted.T, bank, view, *consts)
     return pl.pallas_call(
         functools.partial(last_kernel, zsel, taps // 2),
-        out_shape=arrays((trials, rows, LANES), f32),
-        in_specs=[anywhere] * 11,
+        out_shape=jax.ShapeDtypeStruct((trials, rows, LANES), f32),
+        in_specs=[vmem] * len(kept),
         out_specs=anywhere,
-        scratch_shapes=[
-            *[pltpu.VMEM(a.shape, a.dtype) for a in last],
-            *scratch_consts,
-            pltpu.VMEM((trials - 1, rows, LANES), f32),
-            pltpu.VMEM((rows, LANES), f32),
-            dma((11,)),
-            dma((2, trials - 1)),
-        ],
-        compiler_params=pltpu.CompilerParams(vmem_limit_bytes=LIMIT),
+        scratch_shapes=[pltpu.VMEM((rows, LANES), f32), dma, dma],
+        compiler_params=pltpu.CompilerParams(vmem_limit_bytes=LAST_LIMIT),
         cost_estimate=pl.CostEstimate(
-            flops=6 * macs, bytes_accessed=3 * signal.size * 4, transcendentals=0
+            flops=6 * macs, bytes_accessed=signal.size * 4, transcendentals=0
         ),
         name="last",
-    )(done, *rest[:4], *consts)
+    )(*handed)
 
 
 def on_device(signal, tree_picks, tree_delays, template_bank, template_pick):

time: 380 us -> 374 us (0.984)
  Pallas kernels: 380 us -> 374 us
    pallas_call x1, Pallas kernels: 8.6 us -> 3.41 us  [fused(): pl.pallas_call(functools.partial(last_kernel, zsel, taps // 2), out_shape...]
where the time goes in v4:
time: 374 us
  Pallas kernels  374 us (100%)
    pallas_call x1, Pallas kernels, fused(): pl.pallas_call(functools.partial(fused_kernel, nb, nt, sections, trials,...  370 us

profile of v4, /device:TPU:0, one launch (start us, length us, event | category | flops | bytes accessed | tf_op | source)
XLA Modules:
  0.0 373.9 jit_solution(1600428299931684591)
XLA Ops:
  0.0 370.5 %fused.1 = (f32[15,1024,128]{2,1,0:T(8,128)S(1)}, f32[16,8,512]{2,1,0:T(8,128)S(1)}, f32[16,8,512]{2,1,0:T(8,128)S(1)}, bf16[512,512]{1,0:T(8,128)(2,1)S(1)}, bf...) custom-call(s32[2,8,256]{2,1,0:T(8,128)} %picks_hbm.1, ...), custom_call_target="tpu_custom_call" | custom-call | flops 32212254720 | bytes 25165824 | tf_op jit(solution)/shard_map/fused/pallas_call | solution.py:648
  370.5 3.4 last.1

commit v5 on v4

--- a/solution.py
+++ b/solution.py
@@ -17,7 +17,7 @@
 SUBS = 8
 RADIX = 256
 LIMIT = 56 * 1024 * 1024
-FUSED_LIMIT = 48 * 1024 * 1024
+FUSED_LIMIT = 38 * 1024 * 1024
 LAST_LIMIT = 14 * 1024 * 1024
 AHEAD = 6
 MESH = pl.DeviceIdType.MESH
@@ -340,19 +340,22 @@
     return out.reshape(1, trials, zsel, samples // 2)
 
 
+def rim_pack(sections):
+    return LANES >> (sections * MAXD - 1).bit_length()
+
+
 def fused_kernel(
     nb, nt, sections, trials, zsel, taps,
     picks_hbm, delay_hbm, wanted_hbm, bank_ref, sig_ref, *refs
 ):
     const_refs, refs = refs[:6], refs[6:]
-    power, last_x, band_high, band_low, refs = refs[0], refs[1:3], refs[3], refs[4], refs[5:]
+    power, got, band_high, band_low, refs = refs[0], refs[1:3], refs[3], refs[4], refs[5:]
     consts, sent, refs = refs[:6], refs[6:8], refs[8:]
-    raw, rim, buf_a, buf_b, stage, refs = *refs[:5], refs[5:]
-    got, refs = refs[:2], refs[2:]
+    raw, rim, rim_sent, buf_a, buf_b, stage, refs = *refs[:6], refs[6:]
     bank, reverse, refs = *refs[:2], refs[2:]
     picks_ref, delay_ref, wanted_ref, refs = *refs[:3], refs[3:]
     (
-        one_send, one_recv, two_send, two_recv, rim_sems, stage_sem, load_sems, last_sems,
+        one_send, one_recv, two_send, two_recv, rim_sems, stage_sem, load_sems,
     ) = refs
 
     everyone = nb * nt
@@ -362,6 +365,8 @@
     tiles = span // LANES
     early = range(tiles + 1)
     late = range(tiles + 1, 2 * tiles)
+    pack = rim_pack(sections)
+    share = LANES // pack
     mt, mb = lax.axis_index("tm"), lax.axis_index("band")
     me = mt * nb + mb
 
@@ -460,8 +465,9 @@
                 for i in range(tiles + 1 - c):
                     buf_a[r, :, i * LANES : (i + 1) * LANES] = raw[q, c * tiles + i, rows_of, :]
                 if c == 1:
+                    edges = pltpu.roll(rim[q // pack], (LANES - (q % pack) * share) % LANES, 1)
                     up = pltpu.roll(raw[q, 0, rows_of, :], SUBS - 1, 0)
-                    edge = jnp.broadcast_to(rim[q, ch : ch + 1, :], (SUBS, LANES))
+                    edge = jnp.broadcast_to(edges[ch : ch + 1], (SUBS, LANES))
                     buf_a[r, :, span:] = jnp.where(sub == SUBS - 1, edge, up)
 
         src, dst = buf_a, buf_b
@@ -516,8 +522,17 @@
 
     for i in early:
         first_wait(i)
+
+    @pl.loop(0, nb * blocks // pack)
+    def _(q):
+        packed = raw[q * pack, 0, :SUBS, :]
+        for p in range(1, pack):
+            moved = pltpu.roll(raw[q * pack + p, 0, :SUBS, :], p * share, 1)
+            packed = jnp.where(lane < p * share, packed, moved)
+        rim_sent[q] = packed
+
     rim_copy = pltpu.make_async_remote_copy(
-        raw.at[:, 0, pl.ds(0, SUBS)],
+        rim_sent,
         rim,
         rim_sems.at[0],
         rim_sems.at[1],
@@ -580,13 +595,6 @@
 
     bands_of(last)
     wait_second(1, last)
-    x_copies = [
-        pltpu.make_async_copy(got[c].at[:, last], last_x[c], last_sems.at[c]) for c in range(2)
-    ]
-    for copy in x_copies:
-        copy.start()
-    for copy in x_copies:
-        copy.wait()
     for c in range(2):
         landed(sent[c].at[pl.ds(0, everyone - 1)], two_send.at[c])
 
@@ -600,12 +608,12 @@
 
 
 def last_kernel(zsel, half_taps, *refs):
-    done_ref, early_x, late_x, band_high, band_low = refs[:5]
+    done_ref, got, (band_high, band_low) = refs[0], refs[1:3], refs[3:5]
     consts, out_ref, power, move_sem, sem = refs[5:11], *refs[11:]
     count = done_ref.shape[0]
     move = pltpu.make_async_copy(done_ref, out_ref.at[pl.ds(0, count)], move_sem)
     move.start()
-    x = assemble([early_x[...], late_x[...]], consts)
+    x = assemble([ref[:, count] for ref in got], consts)
 
     def store(where, value):
         power[where, :] = value
@@ -640,7 +648,7 @@
     exchanged = (everyone, trials, SUBS, span)
     kept = [
         pltpu.VMEM((trials - 1, rows, LANES), f32),
-        *[pltpu.VMEM((everyone, SUBS, span), f32)] * 2,
+        *[pltpu.VMEM(exchanged, f32)] * 2,
         *[pltpu.VMEM((2 * RADIX, wide), bf16)] * 2,
         *[pltpu.VMEM(c.shape, c.dtype) for c in consts],
     ]
@@ -652,11 +660,9 @@
         out_specs=[vmem] * len(kept) + [anywhere] * 2,
         scratch_shapes=[
             pltpu.VMEM((nb * blocks, width // LANES, SUBS * SUBS, LANES), f32),
-            pltpu.VMEM((nb * blocks, SUBS, LANES), f32),
+            *[pltpu.VMEM((nb * blocks // rim_pack(sections), SUBS, LANES), f32)] * 2,
             pltpu.VMEM((channels, SUBS, span + LANES), f32),
             pltpu.VMEM((channels, SUBS, span + LANES), f32),
-            pltpu.VMEM(exchanged, f32),
-            pltpu.VMEM(exchanged, f32),
             pltpu.VMEM(exchanged, f32),
             pltpu.VMEM(bank.shape, f32),
             pltpu.VMEM(template_bank.shape[:2] + (RADIX,), f32),
@@ -668,7 +674,6 @@
             dma((2,)),
             dma,
             dma((4 + len(consts),)),
-            dma((2,)),
         ],
         compiler_params=pltpu.CompilerParams(
             collective_id=0, has_side_effects=True, vmem_limit_bytes=FUSED_LIMIT

time: 374 us -> 372 us (level)
  no operation moved by 1% of the time
where the time goes in v5:
time: 372 us
  Pallas kernels  372 us (100%)
    pallas_call x1, Pallas kernels, fused(): pl.pallas_call(functools.partial(fused_kernel, nb, nt, sections, trials,...  368 us

profile of v5, /device:TPU:0, one launch (start us, length us, event | category | flops | bytes accessed | tf_op | source)
XLA Modules:
  0.0 371.8 jit_solution(4247134798010399138)
XLA Ops:
  0.0 368.4 %fused.1 = (f32[15,1024,128]{2,1,0:T(8,128)S(1)}, f32[16,16,8,512]{3,2,1,0:T(8,128)S(1)}, f32[16,16,8,512]{3,2,1,0:T(8,128)S(1)}, bf16[512,512]{1,0:T(8,128)(2,1...) custom-call(s32[2,8,256]{2,1,0:T(8,128)} %picks_hbm.1, ...), custom_call_target="tpu_custom_call" | custom-call | flops 32212254720 | bytes 25165824 | tf_op jit(solution)/shard_map/fused/pallas_call | solution.py:656
  368.4 3.4 last.1

commit v6 on v5

--- a/solution.py
+++ b/solution.py
@@ -494,8 +494,7 @@
     def part_of(c, t):
         return (pl.ds(t, 1), 1 + t) if c else (slice(None), 0)
 
-    def second(c, t, d):
-        e = (me + d) % everyone
+    def second(c, t, e):
         which, at = part_of(c, t)
         return pltpu.make_async_remote_copy(
             sent[c].at[e, which],
@@ -507,9 +506,14 @@
         )
 
     def send_second(c, t):
-        @pl.loop(1, everyone)
-        def _(d):
-            second(c, t, d).start()
+        @pl.loop(0, (nb - 1) * nt)
+        def _(i):
+            b = (mb + 1 + (i // nt + nb // 2 - 1) % (nb - 1)) % nb
+            second(c, t, ((mt + i) % nt) * nb + b).start()
+
+        @pl.loop(1, nt)
+        def _(i):
+            second(c, t, ((mt + i) % nt) * nb + mb).start()
 
         which, at = part_of(c, t)
         pltpu.make_async_copy(

time: 372 us -> 371 us (level)
  no operation moved by 1% of the time
where the time goes in v6:
time: 371 us
  Pallas kernels  371 us (100%)
    pallas_call x1, Pallas kernels, fused(): pl.pallas_call(functools.partial(fused_kernel, nb, nt, sections, trials,...  367 us

profile of v6, /device:TPU:0, one launch (start us, length us, event | category | flops | bytes accessed | tf_op | source)
XLA Modules:
  0.0 370.8 jit_solution(2140278657114174657)
XLA Ops:
  0.0 367.4 %fused.1 = (f32[15,1024,128]{2,1,0:T(8,128)S(1)}, f32[16,16,8,512]{3,2,1,0:T(8,128)S(1)}, f32[16,16,8,512]{3,2,1,0:T(8,128)S(1)}, bf16[512,512]{1,0:T(8,128)(2,1...) custom-call(s32[2,8,256]{2,1,0:T(8,128)} %picks_hbm.1, ...), custom_call_target="tpu_custom_call" | custom-call | flops 32212254720 | bytes 25165824 | tf_op jit(solution)/shard_map/fused/pallas_call | solution.py:660
  367.4 3.4 last.1

commit v7 on v6

--- a/solution.py
+++ b/solution.py
@@ -17,7 +17,7 @@
 SUBS = 8
 RADIX = 256
 LIMIT = 56 * 1024 * 1024
-FUSED_LIMIT = 38 * 1024 * 1024
+FUSED_LIMIT = 41 * 1024 * 1024
 LAST_LIMIT = 14 * 1024 * 1024
 AHEAD = 6
 MESH = pl.DeviceIdType.MESH
@@ -350,12 +350,13 @@
 ):
     const_refs, refs = refs[:6], refs[6:]
     power, got, band_high, band_low, refs = refs[0], refs[1:3], refs[3], refs[4], refs[5:]
-    consts, sent, refs = refs[:6], refs[6:8], refs[8:]
-    raw, rim, rim_sent, buf_a, buf_b, stage, refs = *refs[:6], refs[6:]
+    consts, refs = refs[:6], refs[6:]
+    raw, rim, rim_sent, buf_a, buf_b, refs = *refs[:5], refs[5:]
+    sent, refs = refs[:2], refs[2:]
     bank, reverse, refs = *refs[:2], refs[2:]
     picks_ref, delay_ref, wanted_ref, refs = *refs[:3], refs[3:]
     (
-        one_send, one_recv, two_send, two_recv, rim_sems, stage_sem, load_sems,
+        one_send, one_recv, two_send, two_recv, rim_sems, load_sems,
     ) = refs
 
     everyone = nb * nt
@@ -381,8 +382,6 @@
             barrier, 1, device_id=device((me + d) % everyone), device_id_type=MESH
         )
 
-    pl.semaphore_wait(barrier, everyone - 1)
-
     def slab(i, k):
         return sig_ref.at[:, k, :, pl.ds(i * LANES, LANES)]
 
@@ -407,11 +406,6 @@
     def first_wait(i):
         landed(raw.at[:, i], one_recv.at[i])
 
-    apart = sorted(range(1, nb), key=lambda d: -min(d, nb - d))
-    for i in (*early, *late):
-        for d in apart:
-            first(i, d).start()
-        first_own(i).start()
     loads = [
         pltpu.make_async_copy(a, b, load_sems.at[i])
         for i, (a, b) in enumerate(zip(
@@ -422,6 +416,14 @@
     for load in loads:
         load.start()
 
+    for i in (*early, *late):
+        first_own(i).start()
+    pl.semaphore_wait(barrier, everyone - 1)
+
+    apart = sorted(range(1, nb), key=lambda d: -min(d, nb - d))
+    for i in (*early, *late):
+        for d in apart:
+            first(i, d).start()
     for load in loads[:4]:
         load.wait()
     turn_row = lax.broadcasted_iota(jnp.int32, (taps, RADIX), 0)
@@ -485,11 +487,7 @@
 
             @pl.loop(0, trials, unroll=trials)
             def _(i):
-                merge(src, sections - 1, start + i, stage.at[e], i, tiles)
-
-        copy = pltpu.make_async_copy(stage, sent[c], stage_sem)
-        copy.start()
-        copy.wait()
+                merge(src, sections - 1, start + i, sent[c].at[e], i, tiles)
 
     def part_of(c, t):
         return (pl.ds(t, 1), 1 + t) if c else (slice(None), 0)
@@ -657,17 +655,17 @@
         *[pltpu.VMEM(c.shape, c.dtype) for c in consts],
     ]
     vmem = pl.BlockSpec(memory_space=pltpu.VMEM)
-    *handed, _, _ = pl.pallas_call(
+    handed = pl.pallas_call(
         functools.partial(fused_kernel, nb, nt, sections, trials, zsel, taps),
-        out_shape=kept + [jax.ShapeDtypeStruct(exchanged, f32)] * 2,
+        out_shape=kept,
         in_specs=[anywhere] * 11,
-        out_specs=[vmem] * len(kept) + [anywhere] * 2,
+        out_specs=[vmem] * len(kept),
         scratch_shapes=[
             pltpu.VMEM((nb * blocks, width // LANES, SUBS * SUBS, LANES), f32),
             *[pltpu.VMEM((nb * blocks // rim_pack(sections), SUBS, LANES), f32)] * 2,
             pltpu.VMEM((channels, SUBS, span + LANES), f32),
             pltpu.VMEM((channels, SUBS, span + LANES), f32),
-            pltpu.VMEM(exchanged, f32),
+            *[pltpu.VMEM(exchanged, f32)] * 2,
             pltpu.VMEM(bank.shape, f32),
             pltpu.VMEM(template_bank.shape[:2] + (RADIX,), f32),
             *[pltpu.SMEM(a.shape, jnp.int32) for a in (picks, delays, wanted.T)],
@@ -676,7 +674,6 @@
             dma((2,)),
             dma((1 + trials,)),
             dma((2,)),
-            dma,
             dma((4 + len(consts),)),
         ],
         compiler_params=pltpu.CompilerParams(

time: 371 us -> 371 us (level)
  no operation moved by 1% of the time
where the time goes in v7:
time: 371 us
  Pallas kernels  371 us (100%)
    pallas_call x1, Pallas kernels, fused(): pl.pallas_call(functools.partial(fused_kernel, nb, nt, sections, trials,...  367 us

profile of v7, /device:TPU:0, one launch (start us, length us, event | category | flops | bytes accessed | tf_op | source)
XLA Modules:
  0.0 370.8 jit_solution(6090891908193943089)
XLA Ops:
  0.0 367.4 %fused.1 = (f32[15,1024,128]{2,1,0:T(8,128)S(1)}, f32[16,16,8,512]{3,2,1,0:T(8,128)S(1)}, f32[16,16,8,512]{3,2,1,0:T(8,128)S(1)}, bf16[512,512]{1,0:T(8,128)(2,1...) custom-call(s32[2,8,256]{2,1,0:T(8,128)} %picks_hbm.1, ...), custom_call_target="tpu_custom_call" | custom-call | flops 32212254720 | bytes 25165824 | tf_op jit(solution)/shard_map/fused/pallas_call | solution.py:658
  367.4 3.4 last.1

commit v8 on v6

--- a/solution.py
+++ b/solution.py
@@ -524,8 +524,7 @@
         which, at = part_of(c, t)
         landed(got[c].at[:, which], two_recv.at[at])
 
-    for i in early:
-        first_wait(i)
+    first_wait(0)
 
     @pl.loop(0, nb * blocks // pack)
     def _(q):
@@ -547,6 +546,9 @@
     @pl.when(me > 0)
     def _():
         rim_copy.start()
+
+    for i in early[1:]:
+        first_wait(i)
 
     @pl.when(me == everyone - 1)
     def _():

time: 371 us -> 371 us (level)
  no operation moved by 1% of the time
where the time goes in v8:
time: 371 us
  Pallas kernels  371 us (100%)
    pallas_call x1, Pallas kernels, fused(): pl.pallas_call(functools.partial(fused_kernel, nb, nt, sections, trials,...  367 us

profile of v8, /device:TPU:0, one launch (start us, length us, event | category | flops | bytes accessed | tf_op | source)
XLA Modules:
  0.0 370.6 jit_solution(3213816373771469416)
XLA Ops:
  0.0 367.2 %fused.1 = (f32[15,1024,128]{2,1,0:T(8,128)S(1)}, f32[16,16,8,512]{3,2,1,0:T(8,128)S(1)}, f32[16,16,8,512]{3,2,1,0:T(8,128)S(1)}, bf16[512,512]{1,0:T(8,128)(2,1...) custom-call(s32[2,8,256]{2,1,0:T(8,128)} %picks_hbm.1, ...), custom_call_target="tpu_custom_call" | custom-call | flops 32212254720 | bytes 25165824 | tf_op jit(solution)/shard_map/fused/pallas_call | solution.py:662
  367.2 3.4 last.1
